TPU v7x, 512 devices: a whole 4x8x8 slice. The times are simulated.
512 devices in a mesh: node: 64 (over x, y, core), head: 8 (over z).
Axes of the slice: x: 4, y: 8, z: 8, core: 2. Of those that a mesh axis runs over, the one named last changes fastest.
Arguments:
- features: bfloat16 [262144, 512], P(('node', 'head')), may hold values from -8 to 8
- w_query: bfloat16 [512, 512], replicated, may hold values from -0.25 to 0.25
- w_key_value: bfloat16 [512, 2, 512], replicated, may hold values from -0.25 to 0.25
- edge_local: float32 [512], P('head'), may hold values from 0.5 to 2
- edge_expand: float32 [512], P('head'), may hold values from 0.5 to 2
- local_cols: int32 [2048, 8], P('node'), may hold values from 0 to 35, as said below
- exp_rows: int32 [64, 4, 16], P('node'), may hold values from 0 to 31
- exp_cols: int32 [64, 4, 16], P('node'), may hold values from 0 to 31
Outputs:
- attention: bfloat16 [262144, 512], P(('node', 'head'))
Inputs may be any that keep to these rules, and one draw needn't show every extreme that they name: `local_cols`: the first slot of every row names a tile of the row's own node block, a value from 2 to 33.
All inputs are finite; a program needn't handle non-finite values.
Results may differ from a plain program's by a relative error of at most 0.009.
Values may be sent and summed in bfloat16 or wider, within the bound.
A program may use at most 64 MiB of HBM per device.

v0:
```python
import math

import jax
import jax.numpy as jnp
from jax import lax
from jax.sharding import PartitionSpec as P

HEADS = 8
TILE = 128
HT = 2
MATCH = 4


highest = lax.Precision.HIGHEST


def padded(x, sides, width):
    for axis, dim in sides:
        devices, length = (lax.axis_size(axis), x.shape[dim])
        up = [(i, (i + 1) % devices) for i in range(devices - 1)]
        down = [(j, i) for i, j in up]
        last = lax.slice_in_dim(x, length - width, length, axis=dim)
        first = lax.slice_in_dim(x, 0, width, axis=dim)
        before = lax.ppermute(last, axis, up)
        after = lax.ppermute(first, axis, down)
        x = jnp.concatenate([before, x, after], axis=dim)
    return x


def partner(block, axis, stride):
    count = lax.axis_size(axis)
    route = []
    for low in range(count):
        high = low | 1 << stride
        if high != low and high < count:
            route += [(low, high), (high, low)]
    return lax.ppermute(block, axis, route)


def attend(queries, pair_block, usable):
    head_width = queries.shape[3] // 2
    scores = jnp.einsum("gqhe,gkhe->ghqk", queries, pair_block, preferred_element_type=jnp.float32)
    weights = jnp.exp(jnp.clip(scores, -5.0, 5.0))
    weights = jnp.where(usable[:, None, None, :], weights, jnp.zeros_like(weights))
    denominator = jnp.sum(weights, axis=3)
    combined = jnp.einsum(
        "ghqk,gkhe->gqhe",
        weights.astype(jnp.bfloat16),
        pair_block,
        preferred_element_type=jnp.float32,
    )
    return (combined[:, :, :, head_width:], jnp.transpose(denominator, (0, 2, 1)))


def local_part(queries, extended, columns, first_tile, tile_count, tile_rows, halo_tiles):
    row_count, head_count, double_width = queries.shape
    row_tiles = row_count // tile_rows
    group_size = min(row_tiles, max(1, 512 // tile_rows))
    group_count = row_tiles // group_size
    ext_tiles = extended.reshape(-1, tile_rows, head_count, double_width)
    grouped_queries = queries.reshape(group_count, group_size, tile_rows, head_count, double_width)
    grouped_columns = columns.reshape(group_count, group_size, columns.shape[1])

    def one_group(pair):
        block_queries, block_columns = pair
        picked = ext_tiles[block_columns].reshape(group_size, -1, head_count, double_width)
        global_tile = first_tile + block_columns - halo_tiles
        usable = jnp.logical_and(global_tile >= 0, global_tile < tile_count)
        usable = jnp.repeat(usable, tile_rows, axis=1)
        return attend(block_queries, picked, usable)

    numerator, denominator = lax.map(one_group, (grouped_queries, grouped_columns))
    return (
        numerator.reshape(row_count, head_count, double_width // 2),
        denominator.reshape(row_count, head_count),
    )


def expander_part(queries, key_tiles, row_index):
    row_count, head_count, double_width = queries.shape
    tile_rows = key_tiles.shape[1]
    row_tiles = row_count // tile_rows
    pair_count = key_tiles.shape[0]
    chosen = queries.reshape(row_tiles, tile_rows, head_count, double_width)[row_index]
    pairs = key_tiles.reshape(pair_count, tile_rows, head_count, double_width)
    usable = jnp.ones((pair_count, tile_rows), dtype=jnp.bool_)
    numerator, denominator = attend(chosen, pairs, usable)
    selector = (row_index[None, :] == jnp.arange(row_tiles, dtype=jnp.int32)[:, None]).astype(
        jnp.float32
    )
    numerator = jnp.einsum("te,eqhw->tqhw", selector, numerator, precision=highest)
    denominator = jnp.einsum("te,eqh->tqh", selector, denominator, precision=highest)
    return (
        numerator.reshape(row_count, head_count, double_width // 2),
        denominator.reshape(row_count, head_count),
    )


def widen_query(query_part, heads_here, head_width):
    shaped = query_part.reshape(-1, heads_here, head_width)
    return jnp.concatenate([shaped, jnp.zeros_like(shaped)], axis=2)


def local(features, w_query, w_key_value, edge_local, edge_expand, local_cols, exp_rows, exp_cols):
    groups = lax.axis_size("head")
    node_count = lax.axis_size("node")
    width = features.shape[1]
    head_width = width // HEADS
    local_width = width // groups
    heads_here = local_width // head_width
    scale = 1.0 / math.sqrt(head_width)
    query_cols = w_query.reshape(width, groups, local_width)
    pair_cols = w_key_value.reshape(width, 2, groups, heads_here, head_width)
    pair_cols = jnp.transpose(pair_cols, (0, 2, 3, 1, 4)).reshape(width, groups, 2 * local_width)
    all_cols = jnp.concatenate([query_cols, pair_cols], axis=2).reshape(
        width, groups * 3 * local_width
    )
    projected = jnp.dot(features, all_cols, preferred_element_type=jnp.float32).astype(jnp.bfloat16)
    projected = projected.reshape(-1, groups, 3 * local_width)
    received = lax.all_to_all(projected, "head", split_axis=1, concat_axis=0, tiled=True)
    row_count = received.shape[0]
    received = received.reshape(row_count, 3 * local_width)
    row_tiles = row_count // TILE
    query_wide = lax.optimization_barrier(received[:, :local_width]).astype(jnp.float32)
    local_q = widen_query(
        (query_wide * edge_local * scale).astype(jnp.bfloat16), heads_here, head_width
    )
    expand_q = widen_query(
        (query_wide * edge_expand * scale).astype(jnp.bfloat16), heads_here, head_width
    )
    pair_here = received[:, local_width:]
    extended = padded(pair_here, (("node", 0),), HT * TILE)
    first_tile = lax.axis_index("node") * row_tiles
    numerator, denominator = local_part(
        local_q, extended, local_cols, first_tile, node_count * row_tiles, TILE, HT
    )
    log_count = node_count.bit_length() - 1
    tile_list = []
    row_list = []
    for matching in range(MATCH):
        flip_bit = matching * log_count // 4
        wanted_cols = exp_cols[0, matching]
        partner_pairs = partner(pair_here, "node", flip_bit)
        fetched = partner_pairs.reshape(row_tiles, TILE, 2 * local_width)[wanted_cols]
        tile_list.append(fetched)
        row_list.append(exp_rows[0, matching])
    extra_num, extra_den = expander_part(
        expand_q, jnp.concatenate(tile_list, axis=0), jnp.concatenate(row_list, axis=0)
    )
    result = ((numerator + extra_num) / (denominator + extra_den)[:, :, None]).astype(jnp.bfloat16)
    returned = lax.all_to_all(result, "head", split_axis=0, concat_axis=1, tiled=True)
    return returned.reshape(-1, width)


def solution(mesh):
    return jax.shard_map(
        local,
        mesh=mesh,
        in_specs=(
            P(("node", "head"), None),
            P(),
            P(),
            P("head"),
            P("head"),
            P("node", None),
            P("node", None, None),
            P("node", None, None),
        ),
        out_specs=P(("node", "head"), None),
        check_vma=False,
    )
```

profile of v0, /device:TPU:1, one launch (start us, length us, event | category | flops | bytes accessed | tf_op | source)
XLA Modules:
  0.0 222.9 jit_solution(4957676342415668294)
XLA Ops:
  1.3 2.5 %copy.120 = bf16[512,2,512]{0,2,1:T(8,128)(2,1)S(1)} copy(bf16[512,2,512]{2,1,0:T(2,128)(2,1)} %param.12) | data formatting | bytes 2097152 | tf_op args[2]
  4.0 2.2 convolution_convert_fusion
  6.2 11.0 %all-to-all-start = ((bf16[512,8,192]{0,2,1:T(8,128)(2,1)}), bf16[512,8,192]{0,2,1:T(8,128)(2,1)S(1)}, u32[]{:S(2)}, u32[]{:S(2)}) async-start(bf16[512,8,192]{0,2,1:T(8,128)(2,1)} %bitcast.176), calls=%async_computation | async-start | bytes 3145728 | tf_op jit(solution)/shard_map/all_to_all | solution.py:120
  17.6 37.9 %all-to-all-done = bf16[512,8,192]{0,2,1:T(8,128)(2,1)S(1)} async-done(((bf16[512,8,192]{0,2,1:T(8,128)(2,1)}), bf16[512,8,192]{0,2,1:T(8,128)(2,1)S(1)}, u32[]{:S(2)}, u32[]{:S(2)}) %all-to-all-start) | async-done | bytes 1572896 | tf_op jit(solution)/shard_map/all_to_all | solution.py:120
  56.8 3.1 %collective-permute-start.5 = (bf16[4096,128]{0,1:T(8,128)(2,1)}, bf16[4096,128]{0,1:T(8,128)(2,1)}, u32[]{:S(2)}, u32[]{:S(2)}) collective-permute-start(bf16[4096,128]{0,1:T(8,128)(2,1)} %slice.74), channel_id=1, source_target_pairs={{0,128},{128,0},{8,136},{136,8},{16,144},{144,16},{24,152},{152,24... | collective-permute-start | bytes 3145736 | tf_op jit(solution)/shard_map/ppermute | solution.py:37
  59.9 7.5 %collective-permute-start.4 = (bf16[4096,128]{0,1:T(8,128)(2,1)}, bf16[4096,128]{0,1:T(8,128)(2,1)}, u32[]{:S(2)}, u32[]{:S(2)}) collective-permute-start(bf16[4096,128]{0,1:T(8,128)(2,1)} %slice.74), channel_id=1, source_target_pairs={{0,64},{64,0},{8,72},{72,8},{16,80},{80,16},{24,88},{88,24},{32,96... | collective-permute-start | bytes 3145736 | tf_op jit(solution)/shard_map/ppermute | solution.py:37
  67.4 2.3 %collective-permute-start.3 = (bf16[4096,128]{0,1:T(8,128)(2,1)}, bf16[4096,128]{0,1:T(8,128)(2,1)}, u32[]{:S(2)}, u32[]{:S(2)}) collective-permute-start(bf16[4096,128]{0,1:T(8,128)(2,1)} %slice.74), channel_id=1, source_target_pairs={{0,16},{16,0},{8,24},{24,8},{32,48},{48,32},{40,56},{56,40},{64,80... | collective-permute-start | bytes 3145736 | tf_op jit(solution)/shard_map/ppermute | solution.py:37
  69.7 6.4 %collective-permute-start = (bf16[256,128]{0,1:T(8,128)(2,1)S(1)}, bf16[256,128]{0,1:T(8,128)(2,1)S(1)}, u32[]{:S(2)}, u32[]{:S(2)}) collective-permute-start(bf16[256,128]{0,1:T(8,128)(2,1)S(1)} %get-tuple-element.155), channel_id=1, source_target_pairs={{0,8},{8,16},{16,24},{24,32},{32,40},{40,48},{48,56},{56,64},{64,7... | collective-permute-start | bytes 196616 | tf_op jit(solution)/shard_map/ppermute | solution.py:24
  76.0 1.9 collective-permute-start.1
  79.7 1.8 copy.131
  82.7 51.1 %collective-permute-done = bf16[256,128]{0,1:T(8,128)(2,1)S(1)} collective-permute-done((bf16[256,128]{0,1:T(8,128)(2,1)S(1)}, bf16[256,128]{0,1:T(8,128)(2,1)S(1)}, u32[]{:S(2)}, u32[]{:S(2)}) %collective-permute-start) | collective-permute-done | bytes 65568 | tf_op jit(solution)/shard_map/ppermute | solution.py:24
  133.8 2.1 collective-permute-start.2
  139.1 31.6 %while.14 = (s32[]{:T(128)}, f32[8,4,128,1,64]{2,1,0,3,4:T(4,128)}, f32[8,4,128,1]{2,3,1,0:T(1,128)S(1)}, s32[8,4,8]{2,1,0:T(4,128)S(1)}, bf16[36,128,1,128]{3,1...) while((s32[]{:T(128)}, f32[8,4,128,1,64]{2,1,0,3,4:T(4,128)}, ...), condition=%wide.region_2.3_spmd, body=%wide.region_0.2_spmd.sunk | while | flops 271581952 | bytes 9337909 | solution.py:72
  140.1 1.5 fusion.60
  144.0 1.5 fusion.60
  148.0 1.5 fusion.60
  151.9 1.5 fusion.60
  155.8 1.5 fusion.60
  159.8 1.5 fusion.60
  163.8 1.5 fusion.60
  167.7 1.5 fusion.60
  170.7 1.6 copy.129
  173.0 1.6 copy.128
  176.0 1.6 copy.126
  177.6 1.4 gather_fusion.1
  180.1 2.3 %copy.127 = bf16[4096,128]{1,0:T(8,128)(2,1)} copy(bf16[4096,128]{0,1:T(8,128)(2,1)} %collective-permute-done.3) | data formatting | bytes 2097152 | tf_op jit(solution)/shard_map/ppermute | solution.py:37
  182.4 2.6 %gather_fusion.2 = bf16[16,128,128]{2,1,0:T(8,128)(2,1)} fusion(bf16[32,128,128]{2,1,0:T(8,128)(2,1)} %bitcast.171, s32[1024]{0:T(1024)S(1)} %pad_clamp_fusion.4), kind=kCustom, calls=%fused_computation.2 | custom fusion | bytes 1048640 | tf_op jit(solution)/shard_map/gather | solution.py:144
  187.5 1.6 fusion.14
  190.6 2.1 fusion.19
  193.0 1.9 fusion.30
  197.6 20.4 %all_to_all.30 = bf16[8,2,16384]{2,1,0:T(2,128)(2,1)S(1)} all-to-all(bf16[8,2,16384]{2,1,0:T(2,128)(2,1)S(1)} %reshape.591), channel_id=1, replica_groups=mesh['node'=64,'head'=8] {'head'}, dimensions={0} | all-to-all | bytes 1048576 | tf_op jit(solution)/shard_map/all_to_all | solution.py:151
  219.2 2.3 %copy.137 = bf16[4096,1,64]{0,2,1:T(8,128)(2,1)S(1)} copy(bf16[4096,1,64]{2,1,0:T(2,128)(2,1)S(1)} %reshape.592) | data formatting | bytes 1048576 | tf_op jit(solution)/shard_map/all_to_all | solution.py:151
  (151 shorter events, 40.8 us)
Async XLA Ops:
  0.0 4.0 %copy-start = (bf16[512,512]{1,0:T(8,128)(2,1)S(1)}, bf16[512,512]{1,0:T(8,128)(2,1)}, u32[]{:S(2)}) copy-start(bf16[512,512]{1,0:T(8,128)(2,1)} %param.10) | copy-start | bytes 1572868
  6.2 11.0 %copy-start.2 = (s32[32,8]{0,1:T(8,128)S(1)}, s32[32,8]{0,1:T(8,128)}, u32[]{:S(2)}) copy-start(s32[32,8]{0,1:T(8,128)} %param.15) | copy-start | bytes 3076
  6.2 11.1 %copy-start.3 = (s32[1,4,16]{2,1,0:T(4,128)S(1)}, s32[1,4,16]{2,1,0:T(4,128)}, u32[]{:S(2)}) copy-start(s32[1,4,16]{2,1,0:T(4,128)} %param.16) | copy-start | bytes 772
  6.2 11.3 %copy-start.4 = (s32[1,4,16]{2,1,0:T(4,128)S(1)}, s32[1,4,16]{2,1,0:T(4,128)}, u32[]{:S(2)}) copy-start(s32[1,4,16]{2,1,0:T(4,128)} %param.17) | copy-start | bytes 772
  6.2 49.3 %all-to-all-start = ((bf16[512,8,192]{0,2,1:T(8,128)(2,1)}), bf16[512,8,192]{0,2,1:T(8,128)(2,1)S(1)}, u32[]{:S(2)}, u32[]{:S(2)}) async-start(bf16[512,8,192]{0,2,1:T(8,128)(2,1)} %bitcast.176), calls=%async_computation | async-start | bytes 3145728 | tf_op jit(solution)/shard_map/all_to_all | solution.py:120
  55.6 22.3 %copy-start.5 = (f32[64]{0:T(128)S(1)}, f32[64]{0:T(128)}, u32[]{:S(2)}) copy-start(f32[64]{0:T(128)} %param.13) | copy-start | bytes 772
  55.7 22.3 %copy-start.6 = (f32[64]{0:T(128)S(1)}, f32[64]{0:T(128)}, u32[]{:S(2)}) copy-start(f32[64]{0:T(128)} %param.14) | copy-start | bytes 772
  56.8 113.9 %collective-permute-start.5 = (bf16[4096,128]{0,1:T(8,128)(2,1)}, bf16[4096,128]{0,1:T(8,128)(2,1)}, u32[]{:S(2)}, u32[]{:S(2)}) collective-permute-start(bf16[4096,128]{0,1:T(8,128)(2,1)} %slice.74), channel_id=1, source_target_pairs={{0,128},{128,0},{8,136},{136,8},{16,144},{144,16},{24,152},{152,24... | collective-permute-start | bytes 3145736 | tf_op jit(solution)/shard_map/ppermute | solution.py:37
  59.9 113.1 %collective-permute-start.4 = (bf16[4096,128]{0,1:T(8,128)(2,1)}, bf16[4096,128]{0,1:T(8,128)(2,1)}, u32[]{:S(2)}, u32[]{:S(2)}) collective-permute-start(bf16[4096,128]{0,1:T(8,128)(2,1)} %slice.74), channel_id=1, source_target_pairs={{0,64},{64,0},{8,72},{72,8},{16,80},{80,16},{24,88},{88,24},{32,96... | collective-permute-start | bytes 3145736 | tf_op jit(solution)/shard_map/ppermute | solution.py:37
  67.4 112.8 %collective-permute-start.3 = (bf16[4096,128]{0,1:T(8,128)(2,1)}, bf16[4096,128]{0,1:T(8,128)(2,1)}, u32[]{:S(2)}, u32[]{:S(2)}) collective-permute-start(bf16[4096,128]{0,1:T(8,128)(2,1)} %slice.74), channel_id=1, source_target_pairs={{0,16},{16,0},{8,24},{24,8},{32,48},{48,32},{40,56},{56,40},{64,80... | collective-permute-start | bytes 3145736 | tf_op jit(solution)/shard_map/ppermute | solution.py:37
  69.7 64.1 %collective-permute-start = (bf16[256,128]{0,1:T(8,128)(2,1)S(1)}, bf16[256,128]{0,1:T(8,128)(2,1)S(1)}, u32[]{:S(2)}, u32[]{:S(2)}) collective-permute-start(bf16[256,128]{0,1:T(8,128)(2,1)S(1)} %get-tuple-element.155), channel_id=1, source_target_pairs={{0,8},{8,16},{16,24},{24,32},{32,40},{40,48},{48,56},{56,64},{64,7... | collective-permute-start | bytes 196616 | tf_op jit(solution)/shard_map/ppermute | solution.py:24
  76.0 61.0 %collective-permute-start.1 = (bf16[256,128]{0,1:T(8,128)(2,1)S(1)}, bf16[256,128]{0,1:T(8,128)(2,1)S(1)}, u32[]{:S(2)}, u32[]{:S(2)}) collective-permute-start(bf16[256,128]{0,1:T(8,128)(2,1)S(1)} %get-tuple-element.156), channel_id=1, source_target_pairs={{8,0},{16,8},{24,16},{32,24},{40,32},{48,40},{56,48},{64,56},{72,6... | collective-permute-start | bytes 196616 | tf_op jit(solution)/shard_map/ppermute | solution.py:25
  133.8 42.2 %collective-permute-start.2 = (bf16[4096,128]{0,1:T(8,128)(2,1)}, bf16[4096,128]{0,1:T(8,128)(2,1)}, u32[]{:S(2)}, u32[]{:S(2)}) collective-permute-start(bf16[4096,128]{0,1:T(8,128)(2,1)} %slice.74), channel_id=1, source_target_pairs={{0,8},{8,0},{16,24},{24,16},{32,40},{40,32},{48,56},{56,48},{64,72... | collective-permute-start | bytes 3145736 | tf_op jit(solution)/shard_map/ppermute | solution.py:37
  185.0 2.5 %copy-start.1 = (bf16[64,128,64]{2,1,0:T(8,128)(2,1)S(1)}, bf16[64,128,64]{2,1,0:T(8,128)(2,1)}, u32[]{:S(2)}) copy-start(bf16[64,128,64]{2,1,0:T(8,128)(2,1)} %copy.131) | copy-start | bytes 3145732
where the time goes:
time: 226 us; the launch traced here: 223 us
  waiting for transfers between devices  90.2 us (40%)
  local copies, waits for them, and re-layouts  47.7 us (21%)
  starting transfers between devices  34.2 us (15%)
  matrix products  24.6 us (11%)
  blocking collectives  20.4 us (9%)
  other arithmetic  5 us (2%)
    ppermute x1, waiting for transfers between devices, padded(): before = lax.ppermute(last, axis, up)  51.1 us
    all_to_all x1, waiting for transfers between devices, local(): lax.all_to_all(projected, 'head', split_axis=1, concat_axis=0, tiled=True)  37.9 us
    all_to_all x1, blocking collectives, local(): lax.all_to_all(result, 'head', split_axis=0, concat_axis=1, tiled=True)  20.4 us
    ppermute x4, starting transfers between devices, partner(): return lax.ppermute(block, axis, route)  15 us
    dot_general x9, matrix products, attend(): jnp.einsum('gqhe,gkhe->ghqk', queries, pair_block, preferred_element_type...  13.8 us
    all_to_all x1, starting transfers between devices, local(): lax.all_to_all(projected, 'head', split_axis=1, concat_axis=0, tiled=True)  11 us
    unnamed x26, local copies, waits for them, and re-layouts  10.6 us
    ppermute x4, local copies, waits for them, and re-layouts, partner(): return lax.ppermute(block, axis, route)  7.12 us
  transfers between devices with their start and end apart: 7, of which 3 were waited for; matrix products, arithmetic and copies ran while one was open for 21% of the time, Pallas kernels for 0%

commit v1 on v0

v1 whole, which is shorter than its diff:
```python
import functools
import math

import jax
import jax.numpy as jnp
from jax import lax
from jax.experimental import pallas as pl
from jax.experimental.pallas import tpu as pltpu
from jax.sharding import PartitionSpec as P

HEADS = 8
HDIM = 64
D = 512
TILE = 128
HT = 2
LPR = 8
MATCH = 4
ET = 16
RT = 32
CHUNK = 4
NODES = 64
MESH = pl.DeviceIdType.MESH
F32 = jnp.float32
BF16 = jnp.bfloat16
DISTANCES = (4, 3, 5, 2, 6, 1, 7)
BITS = tuple(m * 6 // 4 for m in range(MATCH))
ROWS_AT = RT * LPR
LAST_AT = ROWS_AT + MATCH * ET
HAS_AT = LAST_AT + MATCH * RT
SAME_AT = HAS_AT + MATCH * RT


def low_lanes(rows):
    return lax.broadcasted_iota(jnp.int32, (rows, TILE), 1) < HDIM


def half_turn(x):
    return pltpu.roll(x, HDIM, 1)


def contract_last(a, b):
    return lax.dot_general(a, b, (((1,), (1,)), ((), ())), preferred_element_type=F32)


def weigh(q, keys):
    return jnp.exp(jnp.clip(contract_last(q, keys), -5.0, 5.0)).astype(BF16)


def with_ones(kv):
    return jnp.where(low_lanes(kv.shape[0]), jnp.ones_like(kv), kv)


def kernel(
    table, feat, w_q, w_kv, edges, cols_out, out,
    send_kv, send_q, kv, halo, vo, q_in, q_local, q_expand, cols_in, cols_smem,
    send_x, kv_x, acc, seg, send_o, o_in,
    kv_ss, kv_rs, q_ss, q_rs, c_ss, c_rs, c_local, h_ss, h_rs, x_ss, x_rs, o_ss, o_rs,
):
    node = lax.axis_index("node")
    me = lax.axis_index("head")

    def around(d):
        return lax.rem(me + d, HEADS)

    def on_z(d):
        return (node, around(d))

    def matched(m):
        return (lax.bitwise_xor(node, jnp.int32(1 << BITS[m])), me)

    def beside(d):
        return (lax.rem(node + d + NODES, NODES), me)

    barrier = pltpu.get_barrier_semaphore()
    greeted = [on_z(d) for d in DISTANCES]
    greeted += [matched(m) for m in range(MATCH)]
    greeted += [beside(1), beside(-1)]
    for device in greeted:
        pl.semaphore_signal(barrier, inc=1, device_id=device, device_id_type=MESH)

    features = feat[...]
    low = low_lanes(CHUNK * TILE)
    for pair in range(HEADS // 2):
        keys = jnp.dot(features, w_kv[:, pair * TILE : (pair + 1) * TILE], preferred_element_type=F32)
        values = jnp.dot(features, w_kv[:, D + pair * TILE : D + (pair + 1) * TILE], preferred_element_type=F32)
        first = jnp.where(low, keys, half_turn(values)).astype(BF16)
        second = jnp.where(low, half_turn(keys), values).astype(BF16)
        send_kv[2 * pair] = first.reshape(CHUNK, TILE, TILE)
        send_kv[2 * pair + 1] = second.reshape(CHUNK, TILE, TILE)

    pl.semaphore_wait(barrier, len(greeted))

    col_copies = []
    for m in range(MATCH):
        copy = pltpu.make_async_remote_copy(
            src_ref=cols_out.at[m], dst_ref=cols_in.at[m], send_sem=c_ss.at[m], recv_sem=c_rs.at[m],
            device_id=matched(m), device_id_type=MESH)
        copy.start()
        col_copies.append(copy)

    def z_copies(src, dst_of, send_sems, recv_sems):
        copies = []
        for i, d in enumerate(DISTANCES):
            copies.append(pltpu.make_async_remote_copy(
                src_ref=src.at[around(d)], dst_ref=dst_of(me), send_sem=send_sems.at[i], recv_sem=recv_sems.at[i],
                device_id=on_z(d), device_id_type=MESH))
        return copies

    kv_copies = z_copies(send_kv, lambda z: kv.at[pl.ds(HT + CHUNK * z, CHUNK)], kv_ss, kv_rs)
    for copy in kv_copies:
        copy.start()
    kv[pl.ds(HT + CHUNK * me, CHUNK)] = send_kv[me]

    half = CHUNK * TILE // 2
    low_half = low_lanes(half)
    for pair in range(HEADS // 2):
        queries = jnp.dot(features, w_q[:, pair * TILE : (pair + 1) * TILE], preferred_element_type=F32)
        top, bottom = queries[:half], queries[half:]
        send_q[2 * pair] = jnp.where(low_half, top, half_turn(bottom)).astype(BF16)
        send_q[2 * pair + 1] = jnp.where(low_half, half_turn(top), bottom).astype(BF16)
    q_copies = z_copies(send_q, lambda z: q_in.at[z], q_ss, q_rs)
    q_in[me] = send_q[me]

    for m in range(MATCH):
        col_copies[m].wait()
        local = pltpu.make_async_copy(cols_in.at[m], cols_smem.at[m], c_local.at[m])
        local.start()
        local.wait()

    for copy in kv_copies:
        copy.wait()

    halo_copies = [
        pltpu.make_async_remote_copy(
            src_ref=kv.at[pl.ds(RT, HT)], dst_ref=halo.at[0], send_sem=h_ss.at[0], recv_sem=h_rs.at[0],
            device_id=beside(1), device_id_type=MESH),
        pltpu.make_async_remote_copy(
            src_ref=kv.at[pl.ds(HT, HT)], dst_ref=halo.at[1], send_sem=h_ss.at[1], recv_sem=h_rs.at[1],
            device_id=beside(-1), device_id_type=MESH),
    ]
    x_copies = {}
    for m in (2, 1, 3, 0):
        def gather(i, carry, m=m):
            send_x[m, i] = kv[HT + cols_smem[m, 0, i]]
            return carry

        lax.fori_loop(0, ET, gather, 0)
        copy = pltpu.make_async_remote_copy(
            src_ref=send_x.at[m], dst_ref=kv_x.at[m], send_sem=x_ss.at[m], recv_sem=x_rs.at[m],
            device_id=matched(m), device_id_type=MESH)
        copy.start()
        x_copies[m] = copy
    for copy in halo_copies:
        copy.start()
    for copy in q_copies:
        copy.start()

    def own_values(i, carry):
        vo[HT + i] = with_ones(kv[HT + i])
        return carry

    lax.fori_loop(0, RT, own_values, 0)

    for copy in halo_copies:
        copy.wait()
    kv[:HT] = halo[0]
    kv[HT + RT :] = halo[1]
    inside = (jnp.where(node > 0, 1.0, 0.0).astype(F32), jnp.where(node < NODES - 1, 1.0, 0.0).astype(F32))
    for i in range(HT):
        vo[i] = (with_ones(kv[i]).astype(F32) * inside[0]).astype(BF16)
        vo[HT + RT + i] = (with_ones(kv[HT + RT + i]).astype(F32) * inside[1]).astype(BF16)

    for copy in q_copies:
        copy.wait()

    def unpack(z, carry):
        packed = q_in[z].astype(F32)
        turned = half_turn(packed)
        for row, target in ((0, q_local), (1, q_expand)):
            scaling = jnp.broadcast_to(edges[row : row + 1, :], (half, TILE))
            for part, source in ((0, packed), (1, turned)):
                scaled = jnp.where(low_half, source * scaling, 0.0).astype(BF16)
                target[pl.ds(CHUNK * z + 2 * part, 2)] = scaled.reshape(2, TILE, TILE)
        return carry

    lax.fori_loop(0, HEADS, unpack, 0)

    def local_tile(t, carry):
        q = q_local[t]
        total = jnp.zeros((TILE, TILE), F32)
        for s in range(0, LPR, 2):
            first, second = table[t * LPR + s], table[t * LPR + s + 1]
            keys = jnp.concatenate([kv[first], kv[second]], axis=0)
            values = jnp.concatenate([vo[first], vo[second]], axis=0)
            total += jnp.dot(weigh(q, keys), values, preferred_element_type=F32)
        acc[t] = total
        return carry

    lax.fori_loop(0, RT, local_tile, 0)

    for m in (0, 3, 1, 2):
        x_copies[m].wait()

        def expander_tile(i, running, m=m):
            q = q_expand[table[ROWS_AT + m * ET + i]]
            keys = kv_x[m, i]
            same = table[SAME_AT + m * ET + i].astype(F32)
            running = running * same + jnp.dot(weigh(q, keys), with_ones(keys), preferred_element_type=F32)
            seg[m, i] = running
            return running

        lax.fori_loop(0, ET, expander_tile, jnp.zeros((TILE, TILE), F32))

    def finish(z, carry):
        tiles = []
        for i in range(CHUNK):
            t = CHUNK * z + i
            total = acc[t]
            for m in range(MATCH):
                has = table[HAS_AT + m * RT + t].astype(F32)
                total += seg[m, table[LAST_AT + m * RT + t]] * has
            tiles.append(total / half_turn(total))
        top = half_turn(jnp.concatenate(tiles[:2], axis=0))
        bottom = jnp.concatenate(tiles[2:], axis=0)
        send_o[z] = jnp.where(low_half, top, bottom).astype(BF16)
        return carry

    o_copies = z_copies(send_o, lambda z: o_in.at[z], o_ss, o_rs)
    for i, d in enumerate(DISTANCES):
        finish(around(d), 0)
        o_copies[i].start()
    finish(me, 0)
    o_in[me] = send_o[me]
    for copy in o_copies:
        copy.wait()
    for pair in range(HEADS // 2):
        a, b = o_in[2 * pair].astype(F32), o_in[2 * pair + 1].astype(F32)
        out[:half, pair * TILE : (pair + 1) * TILE] = jnp.where(low_half, a, half_turn(b)).astype(BF16)
        out[half:, pair * TILE : (pair + 1) * TILE] = jnp.where(low_half, half_turn(a), b).astype(BF16)


def tables(local_cols, exp_rows, exp_cols):
    rows, cols = exp_rows[0], exp_cols[0]
    spot = jnp.arange(ET, dtype=jnp.int32)
    before = (rows[:, None, :] < rows[:, :, None]) | (
        (rows[:, None, :] == rows[:, :, None]) & (spot[None, None, :] < spot[None, :, None]))
    rank = jnp.sum(before.astype(jnp.int32), axis=2)
    place = (rank[:, None, :] == spot[None, :, None]).astype(jnp.int32)
    rows = jnp.sum(place * rows[:, None, :], axis=2)
    cols = jnp.sum(place * cols[:, None, :], axis=2)
    same = jnp.concatenate([jnp.zeros((MATCH, 1), jnp.int32), (rows[:, 1:] == rows[:, :-1]).astype(jnp.int32)], axis=1)
    tiles = jnp.arange(RT, dtype=jnp.int32)
    hits = rows[:, None, :] == tiles[None, :, None]
    has = jnp.max(hits.astype(jnp.int32), axis=2)
    last = jnp.max(jnp.where(hits, spot[None, None, :], 0), axis=2)
    table = jnp.concatenate([part.reshape(-1) for part in (local_cols, rows, last, has, same)])
    cols_out = jnp.zeros((MATCH, 8, TILE), jnp.int32).at[:, 0, :ET].set(cols)
    return table, cols_out


def local(features, w_query, w_key_value, edge_local, edge_expand, local_cols, exp_rows, exp_cols):
    scale = 1.0 / math.sqrt(HDIM)
    edges = jnp.stack([edge_local, edge_expand]) * scale
    edges = jnp.concatenate([edges, edges], axis=1)
    table, cols_out = tables(local_cols, exp_rows, exp_cols)
    vmem = pl.BlockSpec(memory_space=pltpu.VMEM)
    n = len(DISTANCES)
    half = CHUNK * TILE // 2
    dma = pltpu.SemaphoreType.DMA
    return pl.pallas_call(
        kernel,
        name="exphormer",
        out_shape=jax.ShapeDtypeStruct((CHUNK * TILE, D), BF16),
        in_specs=[pl.BlockSpec(memory_space=pltpu.SMEM)] + [vmem] * 5,
        out_specs=vmem,
        scratch_shapes=[
            pltpu.VMEM((HEADS, CHUNK, TILE, TILE), BF16),
            pltpu.VMEM((HEADS, half, TILE), BF16),
            pltpu.VMEM((RT + 2 * HT, TILE, TILE), BF16),
            pltpu.VMEM((2, HT, TILE, TILE), BF16),
        pltpu.VMEM((RT + 2 * HT, TILE, TILE), BF16),
            pltpu.VMEM((HEADS, half, TILE), BF16),
            pltpu.VMEM((RT, TILE, TILE), BF16),
            pltpu.VMEM((RT, TILE, TILE), BF16),
            pltpu.VMEM((MATCH, 8, TILE), jnp.int32),
            pltpu.SMEM((MATCH, 8, TILE), jnp.int32),
            pltpu.VMEM((MATCH, ET, TILE, TILE), BF16),
            pltpu.VMEM((MATCH, ET, TILE, TILE), BF16),
            pltpu.VMEM((RT, TILE, TILE), F32),
            pltpu.VMEM((MATCH, ET, TILE, TILE), F32),
            pltpu.VMEM((HEADS, half, TILE), BF16),
            pltpu.VMEM((HEADS, half, TILE), BF16),
            dma((n,)), dma((n,)), dma((n,)), dma((n,)),
            dma((MATCH,)), dma((MATCH,)), dma((MATCH,)),
            dma((2,)), dma((2,)), dma((MATCH,)), dma((MATCH,)), dma((n,)), dma((n,)),
        ],
        compiler_params=pltpu.CompilerParams(
            collective_id=0, has_side_effects=True, vmem_limit_bytes=56 << 20),
    )(table, features, w_query, w_key_value.reshape(D, 2 * D), edges, cols_out)


def solution(mesh):
    return jax.shard_map(
        local,
        mesh=mesh,
        in_specs=(
            P(("node", "head"), None),
            P(),
            P(),
            P("head"),
            P("head"),
            P("node", None),
            P("node", None, None),
            P("node", None, None),
        ),
        out_specs=P(("node", "head"), None),
        check_vma=False,
    )
```

time: 226 us -> 131 us (0.58); the launches traced: 223 us -> 130 us
  Pallas kernels: 0 us -> 122 us
  waiting for transfers between devices: 90.2 us -> 0 us
  local copies, waits for them, and re-layouts: 47.7 us -> 7.34 us
  starting transfers between devices: 34.2 us -> 0 us
  matrix products: 24.6 us -> 0 us
  blocking collectives: 20.4 us -> 0 us
  other arithmetic: 5 us -> 1.36 us
    pallas_call x0 -> x1, Pallas kernels: none -> 122 us  [local(): pl.pallas_call(kernel, name='exphormer', out_shape=jax.ShapeDtypeStruct((...]
    ppermute x6 -> x0, waiting for transfers between devices: 52.3 us -> none  [the longest x1 51.1 us: padded(): before = lax.ppermute(last, axis, up)]
    all_to_all x1 -> x0, waiting for transfers between devices: 37.9 us -> none  [local(): lax.all_to_all(projected, 'head', split_axis=1, concat_axis=0, tiled=True)]
    dot_general x21 -> x0, matrix products: 24.6 us -> none  [the longest x9 13.8 us: attend(): jnp.einsum('gqhe,gkhe->ghqk', queries, pair_block, preferred_element_type...]
    ppermute x6 -> x0, starting transfers between devices: 23.2 us -> none  [the longest x4 15 us: partner(): return lax.ppermute(block, axis, route)]
    all_to_all x1 -> x0, blocking collectives: 20.4 us -> none  [local(): lax.all_to_all(result, 'head', split_axis=0, concat_axis=1, tiled=True)]
    gather x15 -> x0, local copies, waits for them, and re-layouts: 14.8 us -> none  [the longest x4 6.08 us: local(): partner_pairs.reshape(row_tiles, TILE, 2 * local_width)[wanted_cols]]
    all_to_all x1 -> x0, starting transfers between devices: 11 us -> none  [local(): lax.all_to_all(projected, 'head', split_axis=1, concat_axis=0, tiled=True)]
  transfers between devices with their start and end apart: 7 -> 0, of which waited for: 3 -> 0; matrix products, arithmetic and copies ran while one was open for 21% -> 0% of each run, Pallas kernels for 0% -> 0%
where the time goes in v1:
time: 131 us; the launch traced here: 130 us
  Pallas kernels  122 us (93%)
  local copies, waits for them, and re-layouts  7.34 us (6%)
  other arithmetic  1.36 us (1%)
    pallas_call x1, Pallas kernels, local(): pl.pallas_call(kernel, name='exphormer', out_shape=jax.ShapeDtypeStruct((...  122 us
    unnamed x13, local copies, waits for them, and re-layouts  5.64 us

profile of v1, /device:TPU:1, one launch (start us, length us, event | category | flops | bytes accessed | tf_op | source)
XLA Modules:
  0.0 130.3 jit_solution(18351239695220779705)
XLA Ops:
  0.0 0.0 copy-start.3
  0.0 0.0 copy-start.4
  0.0 0.7 copy-done.3
  0.7 0.0 copy-done.4
  0.7 0.0 copy-start
  0.7 0.7 pad_maximum_fusion.edges
  1.3 0.0 copy-done
  1.4 0.0 copy-start.2
  1.4 0.2 convert_reduce_fusion.1
  1.6 0.5 copy-done.2
  2.0 0.2 select_reduce_fusion
  2.3 0.1 slice_compare_fusion
  2.3 0.1 reshape.80
  2.4 0.1 pad_convert_fusion
  2.5 0.1 reshape.88
  2.6 0.1 convert_reduce_fusion
  2.7 0.1 reshape.82
  2.8 0.1 reshape.81
  2.9 0.0 copy-start.1
  2.9 0.6 scatter.4.cols_out
  3.5 0.1 copy-done.1
  3.6 0.1 copy.12
  3.6 0.1 reshape.79
  3.7 0.7 concatenate.12.table
  4.4 2.5 %copy.14 = bf16[64,8,2,512]{3,1,2,0:T(8,128)(2,1)} copy(bf16[64,8,2,512]{3,2,1,0:T(2,128)(2,1)} %bitcast.10) | data formatting | bytes 2097152
  6.9 121.5 %exphormer.1 = bf16[512,512]{1,0:T(8,128)(2,1)} custom-call(s32[640]{0:T(1024)} %concatenate.12.table, bf16[512,512]{1,0:T(8,128)(2,1)} %feat.1, bf16[512,512]{1,0:T(8,128)(2,1)} %w_q.1, bf16[512,1024]{1,0:T(8,128)(2,1)} %bitcast.9, f32[2,128]{1,0:T(2,128)} %pad_maximum_fusion.edges, s32[4,8,128]{2,1,0:T(8,128)} %scatter.4.cols_out), custom_call_target="tpu_custom_call" | custom-call | tf_op jit(solution)/shard_map/exphormer/pallas_call | solution.py:270
  128.4 1.9 %copy.16 = bf16[512,512]{1,0:T(8,128)(2,1)} copy(bf16[512,512]{1,0:T(8,128)(2,1)} %exphormer.1) | data formatting | bytes 1048576
  (2 shorter events, 0.0 us)
Async XLA Ops:
  0.0 0.7 copy-start.3
  0.0 0.7 copy-start.4
  0.7 0.7 copy-start
  1.4 0.7 copy-start.2
  2.9 0.7 copy-start.1

commit v2 on v1

v2 whole, which is shorter than its diff:
```python
import functools
import math

import jax
import jax.numpy as jnp
from jax import lax
from jax.experimental import pallas as pl
from jax.experimental.pallas import tpu as pltpu
from jax.sharding import PartitionSpec as P

HEADS = 8
HDIM = 64
D = 512
TILE = 128
HT = 2
LPR = 8
MATCH = 4
ET = 16
RT = 32
CHUNK = 4
NODES = 64
MESH = pl.DeviceIdType.MESH
F32 = jnp.float32
BF16 = jnp.bfloat16
DISTANCES = (1, 7, 2, 6, 3, 5, 4)
BITS = tuple(m * 6 // 4 for m in range(MATCH))
NONE = ET
EARLY = 1
LATE = 2


def low_lanes(rows):
    return lax.broadcasted_iota(jnp.int32, (rows, TILE), 1) < HDIM


def half_turn(x):
    return pltpu.roll(x, HDIM, 1)


def contract_last(a, b):
    return lax.dot_general(a, b, (((1,), (1,)), ((), ())), preferred_element_type=F32)


def weigh(q, keys):
    return jnp.exp(jnp.clip(contract_last(q, keys), -5.0, 5.0)).astype(BF16)


def with_ones(kv):
    return jnp.where(low_lanes(kv.shape[0]), jnp.ones_like(kv), kv)


def kernel(
    local_cols, exp_rows, exp_cols, feat, w_q, w_kv, e_local, e_expand, cols_out, out,
    send_kv, send_q, kv, halo, vo, q_in, q_local, q_expand, cols_in, cols_smem,
    send_x, kv_x, kv_y, acc, seg, send_o, o_in, edges, last, prev,
    kv_ss, kv_rs, q_ss, q_rs, c_ss, c_rs, c_local, h_ss, h_rs, x_ss, x_rs, y_ss, y_rs, o_ss, o_rs,
):
    node = lax.axis_index("node")
    me = lax.axis_index("head")
    half = CHUNK * TILE // 2
    low_half = low_lanes(half)
    picked = tuple(m for m in range(MATCH) if m != EARLY)

    def around(d):
        return lax.rem(me + d, HEADS)

    def on_z(d):
        return (node, around(d))

    def matched(m):
        return (lax.bitwise_xor(node, jnp.int32(1 << BITS[m])), me)

    def beside(d):
        return (lax.rem(node + d + NODES, NODES), me)

    def remote(src, dst, send_sem, recv_sem, device):
        return pltpu.make_async_remote_copy(
            src_ref=src, dst_ref=dst, send_sem=send_sem, recv_sem=recv_sem, device_id=device, device_id_type=MESH)

    def z_copies(src, dst, send_sems, recv_sems):
        return [remote(src.at[around(d)], dst, send_sems.at[i], recv_sems.at[i], on_z(d)) for i, d in enumerate(DISTANCES)]

    barrier = pltpu.get_barrier_semaphore()
    greeted = [on_z(d) for d in DISTANCES]
    greeted += [matched(m) for m in range(MATCH)]
    greeted += [beside(1), beside(-1)]
    for device in greeted:
        pl.semaphore_signal(barrier, inc=1, device_id=device, device_id_type=MESH)

    features = feat[...]
    low = low_lanes(CHUNK * TILE)
    wide = 2 * TILE
    for quad in range(HEADS // 4):
        at = quad * wide
        keys = jnp.dot(features, w_kv[:, at : at + wide], preferred_element_type=F32)
        values = jnp.dot(features, w_kv[:, D + at : D + at + wide], preferred_element_type=F32)
        for i in range(2):
            k, v = keys[:, i * TILE : (i + 1) * TILE], values[:, i * TILE : (i + 1) * TILE]
            head = 4 * quad + 2 * i
            send_kv[head] = jnp.where(low, k, half_turn(v)).astype(BF16).reshape(CHUNK, TILE, TILE)
            send_kv[head + 1] = jnp.where(low, half_turn(k), v).astype(BF16).reshape(CHUNK, TILE, TILE)

    pl.semaphore_wait(barrier, len(greeted))

    kv_copies = z_copies(send_kv, kv.at[pl.ds(HT + CHUNK * me, CHUNK)], kv_ss, kv_rs)
    for copy in kv_copies:
        copy.start()
    col_copies = {m: remote(cols_out, cols_in.at[m], c_ss.at[m], c_rs.at[m], matched(m)) for m in picked}
    for copy in col_copies.values():
        copy.start()
    forwards = [remote(send_kv.at[me], kv_y.at[pl.ds(CHUNK * me, CHUNK)], y_ss.at[0], y_rs.at[0], matched(EARLY))]
    forwards[0].start()
    kv[pl.ds(HT + CHUNK * me, CHUNK)] = send_kv[me]

    for pair in range(HEADS // 2):
        queries = jnp.dot(features, w_q[:, pair * TILE : (pair + 1) * TILE], preferred_element_type=F32)
        top, bottom = queries[:half], queries[half:]
        send_q[2 * pair] = jnp.where(low_half, top, half_turn(bottom)).astype(BF16)
        send_q[2 * pair + 1] = jnp.where(low_half, half_turn(top), bottom).astype(BF16)
    q_copies = z_copies(send_q, q_in.at[me], q_ss, q_rs)
    q_in[me] = send_q[me]

    edges[...] = jnp.zeros_like(edges)
    edges[0:1, :HDIM] = e_local[...] * (1.0 / math.sqrt(HDIM))
    edges[1:2, :HDIM] = e_expand[...] * (1.0 / math.sqrt(HDIM))
    for m in range(MATCH):
        seg[m, NONE] = jnp.zeros((TILE, TILE), F32)

    def link(m, carry):
        rows = [exp_rows[0, m, e] for e in range(ET)]
        for e in range(ET):
            found = jnp.int32(NONE)
            for j in range(e):
                found = jnp.where(rows[j] == rows[e], j, found)
            prev[m * ET + e] = found
        return carry

    lax.fori_loop(0, MATCH, link, 0)

    def find(t, carry):
        for m in range(MATCH):
            found = jnp.int32(NONE)
            for e in range(ET):
                found = jnp.where(exp_rows[0, m, e] == t, e, found)
            last[m * RT + t] = found
        return carry

    lax.fori_loop(0, RT, find, 0)

    for i, d in enumerate(DISTANCES):
        kv_copies[i].wait_recv()
        source = around(HEADS - d)
        copy = remote(
            kv.at[pl.ds(HT + CHUNK * source, CHUNK)], kv_y.at[pl.ds(CHUNK * source, CHUNK)],
            y_ss.at[i + 1], y_rs.at[i + 1], matched(EARLY))
        copy.start()
        forwards.append(copy)

    for m in picked:
        col_copies[m].wait()
        local = pltpu.make_async_copy(cols_in.at[m], cols_smem.at[m], c_local.at[m])
        local.start()
        local.wait()

    x_copies = {}

    def send_picked(m):
        for e in range(ET):
            send_x[m, e] = kv[HT + cols_smem[m, m, e]]
        x_copies[m] = remote(send_x.at[m], kv_x.at[m], x_ss.at[m], x_rs.at[m], matched(m))
        x_copies[m].start()

    send_picked(LATE)
    halo_copies = [
        remote(kv.at[pl.ds(RT, HT)], halo.at[0], h_ss.at[0], h_rs.at[0], beside(1)),
        remote(kv.at[pl.ds(HT, HT)], halo.at[1], h_ss.at[1], h_rs.at[1], beside(-1)),
    ]
    for copy in halo_copies:
        copy.start()
    for copy in q_copies:
        copy.start()
    for m in picked:
        if m != LATE:
            send_picked(m)

    def own_values(i, carry):
        vo[HT + i] = with_ones(kv[HT + i])
        return carry

    lax.fori_loop(0, RT, own_values, 0)

    for copy in halo_copies:
        copy.wait()
    kv[:HT] = halo[0]
    kv[HT + RT :] = halo[1]
    inside = (jnp.where(node > 0, 1.0, 0.0).astype(F32), jnp.where(node < NODES - 1, 1.0, 0.0).astype(F32))
    for i in range(HT):
        vo[i] = (with_ones(halo[0, i]).astype(F32) * inside[0]).astype(BF16)
        vo[HT + RT + i] = (with_ones(halo[1, i]).astype(F32) * inside[1]).astype(BF16)

    def unpack(z):
        packed = q_in[z].astype(F32)
        turned = half_turn(packed)
        for row, target in ((0, q_local), (1, q_expand)):
            scaling = jnp.broadcast_to(edges[row : row + 1, :], (half, TILE))
            for part, source in ((0, packed), (1, turned)):
                scaled = jnp.where(low_half, source * scaling, 0.0).astype(BF16)
                target[pl.ds(CHUNK * z + 2 * part, 2)] = scaled.reshape(2, TILE, TILE)

    def local_tiles(z):
        unpack(z)
        for i in range(CHUNK):
            t = CHUNK * z + i
            slots = [local_cols[t, s] for s in range(LPR)]
            keys = jnp.concatenate([kv[c] for c in slots], axis=0)
            values = jnp.concatenate([vo[c] for c in slots], axis=0)
            acc[t] = jnp.dot(weigh(q_local[t], keys), values, preferred_element_type=F32)

    local_tiles(me)
    for i, d in enumerate(DISTANCES):
        q_copies[i].wait()
        local_tiles(around(HEADS - d))

    for copy in forwards:
        copy.wait()

    def expander(m):
        for e in range(ET):
            keys = kv_y[exp_cols[0, m, e]] if m == EARLY else kv_x[m, e]
            q = q_expand[exp_rows[0, m, e]]
            seg[m, e] = jnp.dot(weigh(q, keys), with_ones(keys), preferred_element_type=F32) + seg[m, prev[m * ET + e]]

    order = [EARLY] + [m for m in picked if m != LATE]
    for m in order:
        if m != EARLY:
            x_copies[m].wait()
        expander(m)

    def gather_totals(t, carry):
        total = acc[t]
        for m in order:
            total += seg[m, last[m * RT + t]]
        acc[t] = total
        return carry

    lax.fori_loop(0, RT, gather_totals, 0)
    x_copies[LATE].wait()
    expander(LATE)

    def finish(z):
        tiles = []
        for i in range(CHUNK):
            t = CHUNK * z + i
            total = acc[t] + seg[LATE, last[LATE * RT + t]]
            tiles.append(total / half_turn(total))
        top = half_turn(jnp.concatenate(tiles[:2], axis=0))
        bottom = jnp.concatenate(tiles[2:], axis=0)
        send_o[z] = jnp.where(low_half, top, bottom).astype(BF16)

    o_copies = z_copies(send_o, o_in.at[me], o_ss, o_rs)
    for i in reversed(range(len(DISTANCES))):
        finish(around(DISTANCES[i]))
        o_copies[i].start()
    finish(me)
    o_in[me] = send_o[me]
    for copy in o_copies:
        copy.wait()
    for copy in kv_copies:
        copy.wait_send()
    for pair in range(HEADS // 2):
        a, b = o_in[2 * pair].astype(F32), o_in[2 * pair + 1].astype(F32)
        out[:half, pair * TILE : (pair + 1) * TILE] = jnp.where(low_half, a, half_turn(b)).astype(BF16)
        out[half:, pair * TILE : (pair + 1) * TILE] = jnp.where(low_half, half_turn(a), b).astype(BF16)


def local(features, w_query, w_key_value, edge_local, edge_expand, local_cols, exp_rows, exp_cols):
    smem = pl.BlockSpec(memory_space=pltpu.SMEM)
    vmem = pl.BlockSpec(memory_space=pltpu.VMEM)
    n = len(DISTANCES)
    half = CHUNK * TILE // 2
    dma = pltpu.SemaphoreType.DMA
    return pl.pallas_call(
        kernel,
        name="exphormer",
        out_shape=jax.ShapeDtypeStruct((CHUNK * TILE, D), BF16),
        in_specs=[smem] * 3 + [vmem] * 6,
        out_specs=vmem,
        scratch_shapes=[
            pltpu.VMEM((HEADS, CHUNK, TILE, TILE), BF16),
            pltpu.VMEM((HEADS, half, TILE), BF16),
            pltpu.VMEM((RT + 2 * HT, TILE, TILE), BF16),
            pltpu.VMEM((2, HT, TILE, TILE), BF16),
            pltpu.VMEM((RT + 2 * HT, TILE, TILE), BF16),
            pltpu.VMEM((HEADS, half, TILE), BF16),
            pltpu.VMEM((RT, TILE, TILE), BF16),
            pltpu.VMEM((RT, TILE, TILE), BF16),
            pltpu.VMEM((MATCH, MATCH, ET), jnp.int32),
            pltpu.SMEM((MATCH, MATCH, ET), jnp.int32),
            pltpu.VMEM((MATCH, ET, TILE, TILE), BF16),
            pltpu.VMEM((MATCH, ET, TILE, TILE), BF16),
            pltpu.VMEM((RT, TILE, TILE), BF16),
            pltpu.VMEM((RT, TILE, TILE), F32),
            pltpu.VMEM((MATCH, ET + 1, TILE, TILE), F32),
            pltpu.VMEM((HEADS, half, TILE), BF16),
            pltpu.VMEM((HEADS, half, TILE), BF16),
            pltpu.VMEM((2, TILE), F32),
            pltpu.SMEM((MATCH * RT,), jnp.int32),
            pltpu.SMEM((MATCH * ET,), jnp.int32),
            dma((n,)), dma((n,)), dma((n,)), dma((n,)),
            dma((MATCH,)), dma((MATCH,)), dma((MATCH,)),
            dma((2,)), dma((2,)), dma((MATCH,)), dma((MATCH,)), dma((n + 1,)), dma((n + 1,)), dma((n,)), dma((n,)),
        ],
        compiler_params=pltpu.CompilerParams(
            collective_id=0, has_side_effects=True, vmem_limit_bytes=56 << 20),
    )(local_cols, exp_rows, exp_cols, features, w_query, w_key_value.reshape(D, 2 * D),
      edge_local.reshape(1, HDIM), edge_expand.reshape(1, HDIM), exp_cols.reshape(MATCH, ET))


def solution(mesh):
    return jax.shard_map(
        local,
        mesh=mesh,
        in_specs=(
            P(("node", "head"), None),
            P(),
            P(),
            P("head"),
            P("head"),
            P("node", None),
            P("node", None, None),
            P("node", None, None),
        ),
        out_specs=P(("node", "head"), None),
        check_vma=False,
    )
```

time: 131 us -> 104 us (0.79)
  Pallas kernels: 122 us -> 98.2 us
  local copies, waits for them, and re-layouts: 7.34 us -> 5.69 us
  other arithmetic: 1.36 us -> 0 us
    pallas_call x1, Pallas kernels: 122 us -> 98.2 us  [local(): pl.pallas_call(kernel, name='exphormer', out_shape=jax.ShapeDtypeStruct((...]
    unnamed x13 -> x5, local copies, waits for them, and re-layouts: 5.64 us -> 5.69 us
where the time goes in v2:
time: 104 us
  Pallas kernels  98.2 us (94%)
  local copies, waits for them, and re-layouts  5.69 us (5%)
    pallas_call x1, Pallas kernels, local(): pl.pallas_call(kernel, name='exphormer', out_shape=jax.ShapeDtypeStruct((...  98.2 us
    unnamed x5, local copies, waits for them, and re-layouts  5.69 us

profile of v2, /device:TPU:1, one launch (start us, length us, event | category | flops | bytes accessed | tf_op | source)
XLA Modules:
  0.0 103.9 jit_solution(6514392197461853540)
XLA Ops:
  0.0 0.0 copy-start
  0.0 0.7 copy-done
  0.7 0.7 copy.9.local_cols
  1.4 2.5 %copy.10 = bf16[64,8,2,512]{3,1,2,0:T(8,128)(2,1)} copy(bf16[64,8,2,512]{3,2,1,0:T(2,128)(2,1)} %bitcast.6) | data formatting | bytes 2097152
  3.8 98.2 %exphormer.1 = bf16[512,512]{1,0:T(8,128)(2,1)} custom-call(s32[32,8]{1,0:T(8,128)} %copy.9.local_cols, s32[1,4,16]{2,1,0:T(4,128)} %exp_rows.1, s32[1,4,16]{2,1,0:T(4,128)} %exp_cols.1, bf16[512,512]{1,0:T(8,128)(2,1)} %feat.1, bf16[512,512]{1,0:T(8,128)(2,1)} %w_q.1, bf16[512,1024]{1,0:T(8,128)(2,1)} %bitcast.5, f32[1,64]{1,0:T(1,128)} %bitcast.8, ...), custom_call_target="tpu_custom_call" | custom-call | tf_op jit(solution)/shard_map/exphormer/pallas_call | solution.py:282
  102.0 1.9 %copy.12 = bf16[512,512]{1,0:T(8,128)(2,1)} copy(bf16[512,512]{1,0:T(8,128)(2,1)} %exphormer.1) | data formatting | bytes 1048576
Async XLA Ops:
  0.0 0.7 copy-start

commit v3 on v2

--- a/solution.py
+++ b/solution.py
@@ -17,6 +17,7 @@
 MATCH = 4
 ET = 16
 RT = 32
+PIECES = 4
 CHUNK = 4
 NODES = 64
 MESH = pl.DeviceIdType.MESH
@@ -50,7 +51,8 @@
 
 
 def kernel(
-    local_cols, exp_rows, exp_cols, feat, w_q, w_kv, e_local, e_expand, cols_out, out,
+    local_cols, exp_rows, exp_cols, feat_hbm, w_q_hbm, w_kv_hbm, e_local, e_expand, cols_out, out,
+    feat, w_q, w_kv, in_sem,
     send_kv, send_q, kv, halo, vo, q_in, q_local, q_expand, cols_in, cols_smem,
     send_x, kv_x, kv_y, acc, seg, send_o, o_in, edges, last, prev,
     kv_ss, kv_rs, q_ss, q_rs, c_ss, c_rs, c_local, h_ss, h_rs, x_ss, x_rs, y_ss, y_rs, o_ss, o_rs,
@@ -80,6 +82,13 @@
     def z_copies(src, dst, send_sems, recv_sems):
         return [remote(src.at[around(d)], dst, send_sems.at[i], recv_sems.at[i], on_z(d)) for i, d in enumerate(DISTANCES)]
 
+    loads = []
+    for i in range(PIECES):
+        rows = pl.ds(i * D // PIECES, D // PIECES)
+        for j, (src, dst) in enumerate(((feat_hbm, feat), (w_kv_hbm, w_kv), (w_q_hbm, w_q))):
+            loads.append(pltpu.make_async_copy(src.at[rows], dst.at[rows], in_sem.at[j, i]))
+            loads[-1].start()
+
     barrier = pltpu.get_barrier_semaphore()
     greeted = [on_z(d) for d in DISTANCES]
     greeted += [matched(m) for m in range(MATCH)]
@@ -87,13 +96,16 @@
     for device in greeted:
         pl.semaphore_signal(barrier, inc=1, device_id=device, device_id_type=MESH)
 
+    for copy in loads:
+        copy.wait()
+
     features = feat[...]
     low = low_lanes(CHUNK * TILE)
     wide = 2 * TILE
     for quad in range(HEADS // 4):
         at = quad * wide
-        keys = jnp.dot(features, w_kv[:, at : at + wide], preferred_element_type=F32)
-        values = jnp.dot(features, w_kv[:, D + at : D + at + wide], preferred_element_type=F32)
+        keys = jnp.dot(features, w_kv[:, 0, at : at + wide], preferred_element_type=F32)
+        values = jnp.dot(features, w_kv[:, 1, at : at + wide], preferred_element_type=F32)
         for i in range(2):
             k, v = keys[:, i * TILE : (i + 1) * TILE], values[:, i * TILE : (i + 1) * TILE]
             head = 4 * quad + 2 * i
@@ -108,9 +120,24 @@
     col_copies = {m: remote(cols_out, cols_in.at[m], c_ss.at[m], c_rs.at[m], matched(m)) for m in picked}
     for copy in col_copies.values():
         copy.start()
+    halo_copies = [
+        remote(kv.at[pl.ds(RT, HT)], halo.at[0], h_ss.at[0], h_rs.at[0], beside(1)),
+        remote(kv.at[pl.ds(HT, HT)], halo.at[1], h_ss.at[1], h_rs.at[1], beside(-1)),
+    ]
+
+    def send_halo(chunk):
+        @pl.when(chunk == HEADS - 1)
+        def _():
+            halo_copies[0].start()
+
+        @pl.when(chunk == 0)
+        def _():
+            halo_copies[1].start()
+
     forwards = [remote(send_kv.at[me], kv_y.at[pl.ds(CHUNK * me, CHUNK)], y_ss.at[0], y_rs.at[0], matched(EARLY))]
     forwards[0].start()
     kv[pl.ds(HT + CHUNK * me, CHUNK)] = send_kv[me]
+    send_halo(me)
 
     for pair in range(HEADS // 2):
         queries = jnp.dot(features, w_q[:, pair * TILE : (pair + 1) * TILE], preferred_element_type=F32)
@@ -150,6 +177,7 @@
     for i, d in enumerate(DISTANCES):
         kv_copies[i].wait_recv()
         source = around(HEADS - d)
+        send_halo(source)
         copy = remote(
             kv.at[pl.ds(HT + CHUNK * source, CHUNK)], kv_y.at[pl.ds(CHUNK * source, CHUNK)],
             y_ss.at[i + 1], y_rs.at[i + 1], matched(EARLY))
@@ -171,12 +199,6 @@
         x_copies[m].start()
 
     send_picked(LATE)
-    halo_copies = [
-        remote(kv.at[pl.ds(RT, HT)], halo.at[0], h_ss.at[0], h_rs.at[0], beside(1)),
-        remote(kv.at[pl.ds(HT, HT)], halo.at[1], h_ss.at[1], h_rs.at[1], beside(-1)),
-    ]
-    for copy in halo_copies:
-        copy.start()
     for copy in q_copies:
         copy.start()
     for m in picked:
@@ -211,7 +233,7 @@
         unpack(z)
         for i in range(CHUNK):
             t = CHUNK * z + i
-            slots = [local_cols[t, s] for s in range(LPR)]
+            slots = [local_cols[s, t] for s in range(LPR)]
             keys = jnp.concatenate([kv[c] for c in slots], axis=0)
             values = jnp.concatenate([vo[c] for c in slots], axis=0)
             acc[t] = jnp.dot(weigh(q_local[t], keys), values, preferred_element_type=F32)
@@ -276,6 +298,7 @@
 def local(features, w_query, w_key_value, edge_local, edge_expand, local_cols, exp_rows, exp_cols):
     smem = pl.BlockSpec(memory_space=pltpu.SMEM)
     vmem = pl.BlockSpec(memory_space=pltpu.VMEM)
+    hbm = pl.BlockSpec(memory_space=pltpu.HBM)
     n = len(DISTANCES)
     half = CHUNK * TILE // 2
     dma = pltpu.SemaphoreType.DMA
@@ -283,9 +306,13 @@
         kernel,
         name="exphormer",
         out_shape=jax.ShapeDtypeStruct((CHUNK * TILE, D), BF16),
-        in_specs=[smem] * 3 + [vmem] * 6,
+        in_specs=[smem] * 3 + [hbm] * 3 + [vmem] * 3,
         out_specs=vmem,
         scratch_shapes=[
+            pltpu.VMEM((D, D), BF16),
+            pltpu.VMEM((D, D), BF16),
+            pltpu.VMEM((D, 2, D), BF16),
+            dma((3, PIECES)),
             pltpu.VMEM((HEADS, CHUNK, TILE, TILE), BF16),
             pltpu.VMEM((HEADS, half, TILE), BF16),
             pltpu.VMEM((RT + 2 * HT, TILE, TILE), BF16),
@@ -312,7 +339,7 @@
         ],
         compiler_params=pltpu.CompilerParams(
             collective_id=0, has_side_effects=True, vmem_limit_bytes=56 << 20),
-    )(local_cols, exp_rows, exp_cols, features, w_query, w_key_value.reshape(D, 2 * D),
+    )(local_cols.T, exp_rows, exp_cols, features, w_query, w_key_value,
       edge_local.reshape(1, HDIM), edge_expand.reshape(1, HDIM), exp_cols.reshape(MATCH, ET))
 
 

time: 104 us -> 87.5 us (0.84)
  Pallas kernels: 98.2 us -> 85.4 us
  local copies, waits for them, and re-layouts: 5.69 us -> 1.87 us
    pallas_call x1, Pallas kernels: 98.2 us -> 85.4 us  [local(): pl.pallas_call(kernel, name='exphormer', out_shape=jax.ShapeDtypeStruct((...]
    unnamed x5 -> x1, local copies, waits for them, and re-layouts: 5.69 us -> 1.87 us
where the time goes in v3:
time: 87.5 us; the launch traced here: 87.3 us
  Pallas kernels  85.4 us (98%)
  local copies, waits for them, and re-layouts  1.87 us (2%)
    pallas_call x1, Pallas kernels, local(): pl.pallas_call(kernel, name='exphormer', out_shape=jax.ShapeDtypeStruct((...  85.4 us
    unnamed x1, local copies, waits for them, and re-layouts  1.87 us

profile of v3, /device:TPU:1, one launch (start us, length us, event | category | flops | bytes accessed | tf_op | source)
XLA Modules:
  0.0 87.3 jit_solution(11764464826782333341)
XLA Ops:
  0.0 85.4 %exphormer.1 = bf16[512,512]{1,0:T(8,128)(2,1)} custom-call(s32[8,32]{1,0:T(8,128)} %bitcast.5, s32[1,4,16]{2,1,0:T(4,128)} %exp_rows.1, s32[1,4,16]{2,1,0:T(4,128)} %exp_cols.1, bf16[512,512]{1,0:T(8,128)(2,1)} %feat_hbm.1, bf16[512,512]{1,0:T(8,128)(2,1)} %w_q_hbm.1, bf16[512,2,512]{2,1,0:T(2,128)(2,1)} %w_kv_hbm.1, f32[1,64]{1,0:T(1,128)} %bitcast.6, ...), custom_call_target="tpu_custom_call" | custom-call | tf_op jit(solution)/shard_map/exphormer/pallas_call | solution.py:305
  85.4 1.9 %copy.10 = bf16[512,512]{1,0:T(8,128)(2,1)} copy(bf16[512,512]{1,0:T(8,128)(2,1)} %exphormer.1) | data formatting | bytes 1048576

commit v4 on v3

v4 whole, which is shorter than its diff:
```python
import functools
import math

import jax
import jax.numpy as jnp
from jax import lax
from jax.experimental import pallas as pl
from jax.experimental.pallas import tpu as pltpu
from jax.sharding import PartitionSpec as P

HEADS = 8
HDIM = 64
D = 512
TILE = 128
HT = 2
LPR = 8
MATCH = 4
ET = 16
RT = 32
PIECES = 4
CHUNK = 4
NODES = 64
MESH = pl.DeviceIdType.MESH
F32 = jnp.float32
BF16 = jnp.bfloat16
DISTANCES = (1, 7, 2, 6, 3, 5, 4)
BITS = tuple(m * 6 // 4 for m in range(MATCH))
NONE = ET
EARLY = 1
SENDING = (2, 1, 3, 0)
LAG = 0


def low_lanes(rows):
    return lax.broadcasted_iota(jnp.int32, (rows, TILE), 1) < HDIM


def half_turn(x):
    return pltpu.roll(x, HDIM, 1)


def contract_last(a, b):
    return lax.dot_general(a, b, (((1,), (1,)), ((), ())), preferred_element_type=F32)


def weigh(q, keys):
    return jnp.exp(jnp.clip(contract_last(q, keys), -5.0, 5.0)).astype(BF16)


def kernel(
    local_cols, exp_rows, exp_cols, feat_hbm, w_q_hbm, w_kv_hbm, e_local, e_expand, cols_out, out,
    feat, w_q, w_kv, send_k, send_v, send_q, send_o, k_in, v_in, q_in, o_in, k_early,
    keys, values, turned_values, halo_out, halo_in, q_local, q_expand, cols_in, cols_smem,
    send_kx, send_vx, kx, vx, acc, seg, edges, last, prev,
    in_sem, k_ss, k_rs, v_ss, v_rs, q_ss, q_rs, o_ss, o_rs,
    c_ss, c_rs, c_local, h_ss, h_rs, kx_ss, kx_rs, vx_ss, vx_rs, y_ss, y_rs,
):
    node = lax.axis_index("node")
    me = lax.axis_index("head")
    half = CHUNK * TILE // 2
    low = low_lanes(TILE)
    low_half = low_lanes(half)
    picked = tuple(m for m in SENDING if m != EARLY)

    def around(d):
        return lax.rem(me + d, HEADS)

    def on_z(d):
        return (node, around(d))

    def matched(m):
        return (lax.bitwise_xor(node, jnp.int32(1 << BITS[m])), me)

    def beside(d):
        return (lax.rem(node + d + NODES, NODES), me)

    def remote(src, dst, send_sem, recv_sem, device):
        return pltpu.make_async_remote_copy(
            src_ref=src, dst_ref=dst, send_sem=send_sem, recv_sem=recv_sem, device_id=device, device_id_type=MESH)

    def z_copies(src, dst, send_sems, recv_sems):
        return [remote(src.at[around(d)], dst, send_sems.at[i], recv_sems.at[i], on_z(d)) for i, d in enumerate(DISTANCES)]

    loads = []
    for i in range(PIECES):
        rows = pl.ds(i * D // PIECES, D // PIECES)
        for j, (src, dst) in enumerate(((feat_hbm, feat), (w_kv_hbm, w_kv), (w_q_hbm, w_q))):
            loads.append(pltpu.make_async_copy(src.at[rows], dst.at[rows], in_sem.at[j, i]))
            loads[-1].start()

    barrier = pltpu.get_barrier_semaphore()
    greeted = [on_z(d) for d in DISTANCES]
    greeted += [matched(m) for m in range(MATCH)]
    greeted += [beside(1), beside(-1)]
    for device in greeted:
        pl.semaphore_signal(barrier, inc=1, device_id=device, device_id_type=MESH)

    for copy in loads:
        copy.wait()
    features = feat[...]
    wide = 2 * TILE

    def project(weights_at, target):
        for quad in range(HEADS // 4):
            product = jnp.dot(features, weights_at(quad * wide), preferred_element_type=F32)
            for i in range(2):
                two = product[:, i * TILE : (i + 1) * TILE]
                top, bottom = two[:half], two[half:]
                head = 4 * quad + 2 * i
                target[head] = jnp.where(low_half, top, half_turn(bottom)).astype(BF16).reshape(2, TILE, TILE)
                target[head + 1] = jnp.where(low_half, half_turn(top), bottom).astype(BF16).reshape(2, TILE, TILE)

    project(lambda at: w_kv[:, 0, at : at + wide], send_k)
    pl.semaphore_wait(barrier, len(greeted))
    k_copies = z_copies(send_k, k_in.at[me], k_ss, k_rs)
    for copy in k_copies:
        copy.start()
    forwards = [remote(send_k.at[me], k_early.at[me], y_ss.at[0], y_rs.at[0], matched(EARLY))]
    forwards[0].start()
    col_copies = {m: remote(cols_out, cols_in.at[m], c_ss.at[m], c_rs.at[m], matched(m)) for m in SENDING}
    for copy in col_copies.values():
        copy.start()
    k_in[me] = send_k[me]

    project(lambda at: w_kv[:, 1, at : at + wide], send_v)
    v_copies = z_copies(send_v, v_in.at[me], v_ss, v_rs)
    v_in[me] = send_v[me]

    def spread(packed, target, at):
        target[pl.ds(at, 2)] = packed
        turned = half_turn(packed.reshape(half, TILE).astype(F32)).astype(BF16)
        target[pl.ds(at + 2, 2)] = turned.reshape(2, TILE, TILE)

    def take_keys(z):
        spread(k_in[z], keys, HT + CHUNK * z)

    take_keys(me)
    for i, d in enumerate(DISTANCES):
        k_copies[i].wait_recv()
        if i >= LAG:
            v_copies[i - LAG].start()
        source = around(HEADS - d)
        copy = remote(k_in.at[source], k_early.at[source], y_ss.at[i + 1], y_rs.at[i + 1], matched(EARLY))
        copy.start()
        forwards.append(copy)
        take_keys(source)
    for copy in v_copies[len(DISTANCES) - LAG :]:
        copy.start()

    for m in SENDING:
        col_copies[m].wait()
        local = pltpu.make_async_copy(cols_in.at[m], cols_smem.at[m], c_local.at[m])
        local.start()
        local.wait()

    def send_picked(m, source, target, arrive, send_sems, recv_sems):
        for i in range(ET // 2):
            first, second = cols_smem[m, m, 2 * i], cols_smem[m, m, 2 * i + 1]
            target[m, i] = jnp.where(low, source[HT + first], source[HT + (second ^ 2)])
        copy = remote(target.at[m], arrive.at[m], send_sems.at[m], recv_sems.at[m], matched(m))
        copy.start()
        return copy

    kx_copies = {m: send_picked(m, keys, send_kx, kx, kx_ss, kx_rs) for m in picked}

    project(lambda at: w_q[:, at : at + wide], send_q)
    q_copies = z_copies(send_q, q_in.at[me], q_ss, q_rs)
    q_in[me] = send_q[me]

    for row, source in ((0, e_local), (1, e_expand)):
        scaled = source[...] * (1.0 / math.sqrt(HDIM))
        edges[row : row + 1, :HDIM] = scaled
        edges[row : row + 1, HDIM:] = scaled
    for m in range(MATCH):
        seg[m, NONE] = jnp.zeros((TILE, TILE), F32)

    def link(m, carry):
        rows = [exp_rows[0, m, e] for e in range(ET)]
        for e in range(ET):
            found = jnp.int32(NONE)
            for j in range(e):
                found = jnp.where(rows[j] == rows[e], j, found)
            prev[m * ET + e] = found
        return carry

    lax.fori_loop(0, MATCH, link, 0)

    def find(t, carry):
        for m in range(MATCH):
            found = jnp.int32(NONE)
            for e in range(ET):
                found = jnp.where(exp_rows[0, m, e] == t, e, found)
            last[m * RT + t] = found
        return carry

    lax.fori_loop(0, RT, find, 0)

    halo_copies = [
        remote(halo_out.at[0], halo_in.at[0], h_ss.at[0], h_rs.at[0], beside(1)),
        remote(halo_out.at[1], halo_in.at[1], h_ss.at[1], h_rs.at[1], beside(-1)),
    ]

    def take_values(z):
        at = HT + CHUNK * z
        spread(v_in[z], turned_values, at)
        for i in range(CHUNK):
            values[at + i] = jnp.where(low, 1.0, turned_values[at + (i ^ 2)]).astype(BF16)

        def send_halo(which, first):
            for i in range(HT):
                halo_out[which, i] = jnp.where(low, keys[HT + first + i], turned_values[HT + ((first + i) ^ 2)])
            halo_copies[which].start()

        @pl.when(z == HEADS - 1)
        def _():
            send_halo(0, RT - HT)

        @pl.when(z == 0)
        def _():
            send_halo(1, 0)

    take_values(me)
    for i, d in enumerate(DISTANCES):
        v_copies[i].wait_recv()
        if i >= LAG:
            q_copies[i - LAG].start()
        take_values(around(HEADS - d))
    for copy in q_copies[len(DISTANCES) - LAG :]:
        copy.start()

    vx_copies = {m: send_picked(m, turned_values, send_vx, vx, vx_ss, vx_rs) for m in SENDING}

    for copy in halo_copies:
        copy.wait()
    inside = (jnp.where(node > 0, 1.0, 0.0).astype(F32), jnp.where(node < NODES - 1, 1.0, 0.0).astype(F32))
    for which, at in ((0, 0), (1, HT + RT)):
        for i in range(HT):
            keys[at + i] = halo_in[which, i]
            values[at + i] = (jnp.where(low, 1.0, halo_in[which, i].astype(F32)) * inside[which]).astype(BF16)

    def unpack(z):
        packed = q_in[z].reshape(half, TILE).astype(F32)
        turned = half_turn(packed)
        zeros = jnp.zeros((half, TILE), BF16)
        for row in range(2):
            scaling = jnp.broadcast_to(edges[row : row + 1, :], (half, TILE))
            for part, source in ((0, packed), (1, turned)):
                scaled = (source * scaling).astype(BF16)
                lower = jnp.where(low_half, scaled, zeros).reshape(2, TILE, TILE)
                if row == 0:
                    q_local[pl.ds(CHUNK * z + 2 * part, 2)] = lower
                else:
                    upper = jnp.where(low_half, zeros, scaled).reshape(2, TILE, TILE)
                    q_expand[0, pl.ds(CHUNK * z + 2 * part, 2)] = lower
                    q_expand[1, pl.ds(CHUNK * z + 2 * (1 - part), 2)] = upper

    def local_tiles(z):
        unpack(z)
        for i in range(CHUNK):
            t = CHUNK * z + i
            slots = [local_cols[s, t] for s in range(LPR)]
            some_keys = jnp.concatenate([keys[c] for c in slots], axis=0)
            some_values = jnp.concatenate([values[c] for c in slots], axis=0)
            acc[t] = jnp.dot(weigh(q_local[t], some_keys), some_values, preferred_element_type=F32)

    local_tiles(me)
    for i, d in enumerate(DISTANCES):
        q_copies[i].wait_recv()
        local_tiles(around(HEADS - d))

    def expander(m):
        for e in range(ET):
            row, i, upper = exp_rows[0, m, e], e // 2, e % 2
            if m == EARLY:
                col = exp_cols[0, m, e]
                weights = weigh(q_expand[(col // 2) % 2, row], k_early[col // CHUNK, col % 2])
            else:
                weights = weigh(q_expand[upper, row], kx[m, i])
            pair = vx[m, i]
            if upper:
                part = jnp.dot(weights, jnp.where(low, jnp.ones_like(pair), pair), preferred_element_type=F32)
            else:
                part = half_turn(jnp.dot(weights, jnp.where(low, pair, jnp.ones_like(pair)), preferred_element_type=F32))
            seg[m, e] = part + seg[m, prev[m * ET + e]]

    for copy in forwards:
        copy.wait()
    order = tuple(reversed(SENDING))
    for m in order:
        if m == order[-1]:
            def gather_totals(t, carry):
                total = acc[t]
                for m in order[:-1]:
                    total += seg[m, last[m * RT + t]]
                acc[t] = total
                return carry

            lax.fori_loop(0, RT, gather_totals, 0)
        if m != EARLY:
            kx_copies[m].wait()
        vx_copies[m].wait()
        expander(m)

    def finish(z):
        tiles = []
        for i in range(CHUNK):
            t = CHUNK * z + i
            total = acc[t] + seg[order[-1], last[order[-1] * RT + t]]
            tiles.append(total / half_turn(total))
        top = half_turn(jnp.concatenate(tiles[:2], axis=0))
        bottom = jnp.concatenate(tiles[2:], axis=0)
        send_o[z] = jnp.where(low_half, top, bottom).astype(BF16).reshape(2, TILE, TILE)

    o_copies = z_copies(send_o, o_in.at[me], o_ss, o_rs)
    for i in reversed(range(len(DISTANCES))):
        finish(around(DISTANCES[i]))
        o_copies[i].start()
    finish(me)
    o_in[me] = send_o[me]
    for copy in o_copies:
        copy.wait()
    for copy in k_copies + v_copies + q_copies:
        copy.wait_send()
    for pair in range(HEADS // 2):
        a, b = (o_in[2 * pair + i].reshape(half, TILE).astype(F32) for i in range(2))
        out[:half, pair * TILE : (pair + 1) * TILE] = jnp.where(low_half, a, half_turn(b)).astype(BF16)
        out[half:, pair * TILE : (pair + 1) * TILE] = jnp.where(low_half, half_turn(a), b).astype(BF16)


def local(features, w_query, w_key_value, edge_local, edge_expand, local_cols, exp_rows, exp_cols):
    smem = pl.BlockSpec(memory_space=pltpu.SMEM)
    vmem = pl.BlockSpec(memory_space=pltpu.VMEM)
    hbm = pl.BlockSpec(memory_space=pltpu.HBM)
    n = len(DISTANCES)
    dma = pltpu.SemaphoreType.DMA
    packed = pltpu.VMEM((HEADS, 2, TILE, TILE), BF16)
    block = pltpu.VMEM((RT + 2 * HT, TILE, TILE), BF16)
    pairs = pltpu.VMEM((MATCH, ET // 2, TILE, TILE), BF16)
    halo = pltpu.VMEM((2, HT, TILE, TILE), BF16)
    return pl.pallas_call(
        kernel,
        name="exphormer",
        out_shape=jax.ShapeDtypeStruct((CHUNK * TILE, D), BF16),
        in_specs=[smem] * 3 + [hbm] * 3 + [vmem] * 3,
        out_specs=vmem,
        scratch_shapes=[
            pltpu.VMEM((D, D), BF16),
            pltpu.VMEM((D, D), BF16),
            pltpu.VMEM((D, 2, D), BF16),
            packed, packed, packed, packed,
            packed, packed, packed, packed, packed,
            block, block, block,
            halo, halo,
            pltpu.VMEM((RT, TILE, TILE), BF16),
            pltpu.VMEM((2, RT, TILE, TILE), BF16),
            pltpu.VMEM((MATCH, MATCH, ET), jnp.int32),
            pltpu.SMEM((MATCH, MATCH, ET), jnp.int32),
            pairs, pairs, pairs, pairs,
            pltpu.VMEM((RT, TILE, TILE), F32),
            pltpu.VMEM((MATCH, ET + 1, TILE, TILE), F32),
            pltpu.VMEM((2, TILE), F32),
            pltpu.SMEM((MATCH * RT,), jnp.int32),
            pltpu.SMEM((MATCH * ET,), jnp.int32),
            dma((3, PIECES)),
            dma((n,)), dma((n,)), dma((n,)), dma((n,)), dma((n,)), dma((n,)), dma((n,)), dma((n,)),
            dma((MATCH,)), dma((MATCH,)), dma((MATCH,)), dma((2,)), dma((2,)),
            dma((MATCH,)), dma((MATCH,)), dma((MATCH,)), dma((MATCH,)), dma((n + 1,)), dma((n + 1,)),
        ],
        compiler_params=pltpu.CompilerParams(
            collective_id=0, has_side_effects=True, vmem_limit_bytes=56 << 20),
    )(local_cols.T, exp_rows, exp_cols, features, w_query, w_key_value,
      edge_local.reshape(1, HDIM), edge_expand.reshape(1, HDIM), exp_cols.reshape(MATCH, ET))


def solution(mesh):
    return jax.shard_map(
        local,
        mesh=mesh,
        in_specs=(
            P(("node", "head"), None),
            P(),
            P(),
            P("head"),
            P("head"),
            P("node", None),
            P("node", None, None),
            P("node", None, None),
        ),
        out_specs=P(("node", "head"), None),
        check_vma=False,
    )
```

time: 87.5 us -> 85.6 us (0.978)
  Pallas kernels: 85.4 us -> 83.5 us
    pallas_call x1, Pallas kernels: 85.4 us -> 83.5 us  [local(): pl.pallas_call(kernel, name='exphormer', out_shape=jax.ShapeDtypeStruct((...]
where the time goes in v4:
time: 85.6 us; the launch traced here: 85.4 us
  Pallas kernels  83.5 us (98%)
  local copies, waits for them, and re-layouts  1.87 us (2%)
    pallas_call x1, Pallas kernels, local(): pl.pallas_call(kernel, name='exphormer', out_shape=jax.ShapeDtypeStruct((...  83.5 us
    unnamed x1, local copies, waits for them, and re-layouts  1.87 us

profile of v4, /device:TPU:1, one launch (start us, length us, event | category | flops | bytes accessed | tf_op | source)
XLA Modules:
  0.0 85.4 jit_solution(175673656790319572)
XLA Ops:
  0.0 83.5 %exphormer.1 = bf16[512,512]{1,0:T(8,128)(2,1)} custom-call(s32[8,32]{1,0:T(8,128)} %bitcast.5, s32[1,4,16]{2,1,0:T(4,128)} %exp_rows.1, s32[1,4,16]{2,1,0:T(4,128)} %exp_cols.1, bf16[512,512]{1,0:T(8,128)(2,1)} %feat_hbm.1, bf16[512,512]{1,0:T(8,128)(2,1)} %w_q_hbm.1, bf16[512,2,512]{2,1,0:T(2,128)(2,1)} %w_kv_hbm.1, f32[1,64]{1,0:T(1,128)} %bitcast.6, ...), custom_call_target="tpu_custom_call" | custom-call | tf_op jit(solution)/shard_map/exphormer/pallas_call | solution.py:340
  83.5 1.9 %copy.10 = bf16[512,512]{1,0:T(8,128)(2,1)} copy(bf16[512,512]{1,0:T(8,128)(2,1)} %exphormer.1) | data formatting | bytes 1048576

commit v5 on v4

--- a/solution.py
+++ b/solution.py
@@ -23,12 +23,17 @@
 MESH = pl.DeviceIdType.MESH
 F32 = jnp.float32
 BF16 = jnp.bfloat16
-DISTANCES = (1, 7, 2, 6, 3, 5, 4)
-BITS = tuple(m * 6 // 4 for m in range(MATCH))
 NONE = ET
 EARLY = 1
 SENDING = (2, 1, 3, 0)
-LAG = 0
+TAKING = 3
+
+
+STEPS = HEADS - 1
+
+
+def distance(i):
+    return i // 2 + 1 + (i % 2) * (HEADS - 2 - 2 * (i // 2))
 
 
 def low_lanes(rows):
@@ -50,7 +55,7 @@
 def kernel(
     local_cols, exp_rows, exp_cols, feat_hbm, w_q_hbm, w_kv_hbm, e_local, e_expand, cols_out, out,
     feat, w_q, w_kv, send_k, send_v, send_q, send_o, k_in, v_in, q_in, o_in, k_early,
-    keys, values, turned_values, halo_out, halo_in, q_local, q_expand, cols_in, cols_smem,
+    keys, values, turned_values, halo_out, halo_in, q_local, q_expand, cols_in, cols_smem, keys_early,
     send_kx, send_vx, kx, vx, acc, seg, edges, last, prev,
     in_sem, k_ss, k_rs, v_ss, v_rs, q_ss, q_rs, o_ss, o_rs,
     c_ss, c_rs, c_local, h_ss, h_rs, kx_ss, kx_rs, vx_ss, vx_rs, y_ss, y_rs,
@@ -69,7 +74,7 @@
         return (node, around(d))
 
     def matched(m):
-        return (lax.bitwise_xor(node, jnp.int32(1 << BITS[m])), me)
+        return (lax.bitwise_xor(node, jnp.left_shift(jnp.int32(1), m * 3 // 2)), me)
 
     def beside(d):
         return (lax.rem(node + d + NODES, NODES), me)
@@ -78,52 +83,65 @@
         return pltpu.make_async_remote_copy(
             src_ref=src, dst_ref=dst, send_sem=send_sem, recv_sem=recv_sem, device_id=device, device_id_type=MESH)
 
-    def z_copies(src, dst, send_sems, recv_sems):
-        return [remote(src.at[around(d)], dst, send_sems.at[i], recv_sems.at[i], on_z(d)) for i, d in enumerate(DISTANCES)]
+    def z_copy(i, src, dst, sems):
+        d = distance(i)
+        return remote(src.at[around(d)], dst.at[me], sems[0].at[i], sems[1].at[i], on_z(d))
+
+    def steps(body):
+        def step(i, carry):
+            body(i, around(HEADS - distance(i)))
+            return carry
+
+        lax.fori_loop(0, STEPS, step, 0)
+
+    k_sems, v_sems, q_sems, o_sems = (k_ss, k_rs), (v_ss, v_rs), (q_ss, q_rs), (o_ss, o_rs)
 
     loads = []
-    for i in range(PIECES):
-        rows = pl.ds(i * D // PIECES, D // PIECES)
-        for j, (src, dst) in enumerate(((feat_hbm, feat), (w_kv_hbm, w_kv), (w_q_hbm, w_q))):
+    for j, (src, dst) in enumerate(((feat_hbm, feat), (w_kv_hbm, w_kv), (w_q_hbm, w_q))):
+        for i in range(PIECES):
+            rows = pl.ds(i * D // PIECES, D // PIECES)
             loads.append(pltpu.make_async_copy(src.at[rows], dst.at[rows], in_sem.at[j, i]))
             loads[-1].start()
 
     barrier = pltpu.get_barrier_semaphore()
-    greeted = [on_z(d) for d in DISTANCES]
+    greeted = [on_z(d) for d in range(1, HEADS)]
     greeted += [matched(m) for m in range(MATCH)]
     greeted += [beside(1), beside(-1)]
     for device in greeted:
         pl.semaphore_signal(barrier, inc=1, device_id=device, device_id_type=MESH)
 
-    for copy in loads:
+    for copy in loads[: 2 * PIECES]:
         copy.wait()
     features = feat[...]
     wide = 2 * TILE
 
     def project(weights_at, target):
-        for quad in range(HEADS // 4):
-            product = jnp.dot(features, weights_at(quad * wide), preferred_element_type=F32)
+        def quarter(quad, carry):
+            product = jnp.dot(features, weights_at(pl.ds(pl.multiple_of(quad * wide, wide), wide)), preferred_element_type=F32)
             for i in range(2):
                 two = product[:, i * TILE : (i + 1) * TILE]
                 top, bottom = two[:half], two[half:]
                 head = 4 * quad + 2 * i
                 target[head] = jnp.where(low_half, top, half_turn(bottom)).astype(BF16).reshape(2, TILE, TILE)
                 target[head + 1] = jnp.where(low_half, half_turn(top), bottom).astype(BF16).reshape(2, TILE, TILE)
-
-    project(lambda at: w_kv[:, 0, at : at + wide], send_k)
+            return carry
+
+        lax.fori_loop(0, HEADS // 4, quarter, 0)
+
+    project(lambda at: w_kv[:, 0, at], send_k)
     pl.semaphore_wait(barrier, len(greeted))
-    k_copies = z_copies(send_k, k_in.at[me], k_ss, k_rs)
-    for copy in k_copies:
-        copy.start()
-    forwards = [remote(send_k.at[me], k_early.at[me], y_ss.at[0], y_rs.at[0], matched(EARLY))]
-    forwards[0].start()
+    steps(lambda i, source: z_copy(i, send_k, k_in, k_sems).start())
+
+    def forward(i, src, z):
+        return remote(src.at[z], k_early.at[z], y_ss.at[i], y_rs.at[i], matched(EARLY))
+
+    forward(STEPS, send_k, me).start()
     col_copies = {m: remote(cols_out, cols_in.at[m], c_ss.at[m], c_rs.at[m], matched(m)) for m in SENDING}
     for copy in col_copies.values():
         copy.start()
     k_in[me] = send_k[me]
 
-    project(lambda at: w_kv[:, 1, at : at + wide], send_v)
-    v_copies = z_copies(send_v, v_in.at[me], v_ss, v_rs)
+    project(lambda at: w_kv[:, 1, at], send_v)
     v_in[me] = send_v[me]
 
     def spread(packed, target, at):
@@ -135,17 +153,14 @@
         spread(k_in[z], keys, HT + CHUNK * z)
 
     take_keys(me)
-    for i, d in enumerate(DISTANCES):
-        k_copies[i].wait_recv()
-        if i >= LAG:
-            v_copies[i - LAG].start()
-        source = around(HEADS - d)
-        copy = remote(k_in.at[source], k_early.at[source], y_ss.at[i + 1], y_rs.at[i + 1], matched(EARLY))
-        copy.start()
-        forwards.append(copy)
+
+    def on_keys(i, source):
+        z_copy(i, send_k, k_in, k_sems).wait_recv()
+        z_copy(i, send_v, v_in, v_sems).start()
+        forward(i, k_in, source).start()
         take_keys(source)
-    for copy in v_copies[len(DISTANCES) - LAG :]:
-        copy.start()
+
+    steps(on_keys)
 
     for m in SENDING:
         col_copies[m].wait()
@@ -153,18 +168,24 @@
         local.start()
         local.wait()
 
-    def send_picked(m, source, target, arrive, send_sems, recv_sems):
+    def kx_copy(m):
+        return remote(send_kx.at[m], kx.at[m], kx_ss.at[m], kx_rs.at[m], matched(m))
+
+    def vx_copy(m):
+        return remote(send_vx.at[m], vx.at[m], vx_ss.at[m], vx_rs.at[m], matched(m))
+
+    def pick(m, source, target):
         for i in range(ET // 2):
             first, second = cols_smem[m, m, 2 * i], cols_smem[m, m, 2 * i + 1]
             target[m, i] = jnp.where(low, source[HT + first], source[HT + (second ^ 2)])
-        copy = remote(target.at[m], arrive.at[m], send_sems.at[m], recv_sems.at[m], matched(m))
-        copy.start()
-        return copy
-
-    kx_copies = {m: send_picked(m, keys, send_kx, kx, kx_ss, kx_rs) for m in picked}
-
-    project(lambda at: w_q[:, at : at + wide], send_q)
-    q_copies = z_copies(send_q, q_in.at[me], q_ss, q_rs)
+
+    for m in picked:
+        pick(m, keys, send_kx)
+        kx_copy(m).start()
+
+    for copy in loads[2 * PIECES :]:
+        copy.wait()
+    project(lambda at: w_q[:, at], send_q)
     q_in[me] = send_q[me]
 
     for row, source in ((0, e_local), (1, e_expand)):
@@ -220,23 +241,29 @@
             send_halo(1, 0)
 
     take_values(me)
-    for i, d in enumerate(DISTANCES):
-        v_copies[i].wait_recv()
-        if i >= LAG:
-            q_copies[i - LAG].start()
-        take_values(around(HEADS - d))
-    for copy in q_copies[len(DISTANCES) - LAG :]:
-        copy.start()
-
-    vx_copies = {m: send_picked(m, turned_values, send_vx, vx, vx_ss, vx_rs) for m in SENDING}
-
-    for copy in halo_copies:
-        copy.wait()
-    inside = (jnp.where(node > 0, 1.0, 0.0).astype(F32), jnp.where(node < NODES - 1, 1.0, 0.0).astype(F32))
-    for which, at in ((0, 0), (1, HT + RT)):
-        for i in range(HT):
-            keys[at + i] = halo_in[which, i]
-            values[at + i] = (jnp.where(low, 1.0, halo_in[which, i].astype(F32)) * inside[which]).astype(BF16)
+
+    def on_values(i, source):
+        z_copy(i, send_v, v_in, v_sems).wait_recv()
+        z_copy(i, send_q, q_in, q_sems).start()
+        take_values(source)
+
+    steps(on_values)
+
+    for m in SENDING:
+        pick(m, turned_values, send_vx)
+        vx_copy(m).start()
+
+    forward(STEPS, send_k, me).wait()
+    spread(k_early[me], keys_early, CHUNK * me)
+
+    def on_forwarded(i, source):
+        forward(i, k_in, source).wait()
+        spread(k_early[source], keys_early, CHUNK * source)
+
+    steps(on_forwarded)
+    for i in range(ET // 2):
+        one, other = exp_cols[0, EARLY, 2 * i], exp_cols[0, EARLY, 2 * i + 1]
+        kx[EARLY, i] = jnp.where(low, keys_early[one], keys_early[other ^ 2])
 
     def unpack(z):
         packed = q_in[z].reshape(half, TILE).astype(F32)
@@ -255,7 +282,6 @@
                     q_expand[1, pl.ds(CHUNK * z + 2 * (1 - part), 2)] = upper
 
     def local_tiles(z):
-        unpack(z)
         for i in range(CHUNK):
             t = CHUNK * z + i
             slots = [local_cols[s, t] for s in range(LPR)]
@@ -263,64 +289,95 @@
             some_values = jnp.concatenate([values[c] for c in slots], axis=0)
             acc[t] = jnp.dot(weigh(q_local[t], some_keys), some_values, preferred_element_type=F32)
 
-    local_tiles(me)
-    for i, d in enumerate(DISTANCES):
-        q_copies[i].wait_recv()
-        local_tiles(around(HEADS - d))
-
-    def expander(m):
+    for copy in halo_copies:
+        copy.wait()
+    inside = (jnp.where(node > 0, 1.0, 0.0).astype(F32), jnp.where(node < NODES - 1, 1.0, 0.0).astype(F32))
+    for which, at in ((0, 0), (1, HT + RT)):
+        for i in range(HT):
+            keys[at + i] = halo_in[which, i]
+            values[at + i] = (jnp.where(low, 1.0, halo_in[which, i].astype(F32)) * inside[which]).astype(BF16)
+
+    def on_queries(k, carry):
+        i = jnp.maximum(k - 1, 0)
+
+        @pl.when(k > 0)
+        def _():
+            z_copy(i, send_q, q_in, q_sems).wait_recv()
+
+        z = jnp.where(k > 0, around(HEADS - distance(i)), me)
+        unpack(z)
+        local_tiles(z)
+        return carry
+
+    lax.fori_loop(0, HEADS, on_queries, 0)
+
+    def expander(k, carry):
+        m = TAKING * k % MATCH
+
+        @pl.when(k == MATCH - 1)
+        def _():
+            lax.fori_loop(0, RT, gather_totals, 0)
+
+        @pl.when(m != EARLY)
+        def _():
+            kx_copy(m).wait()
+
+        vx_copy(m).wait()
+        parts = []
         for e in range(ET):
-            row, i, upper = exp_rows[0, m, e], e // 2, e % 2
-            if m == EARLY:
-                col = exp_cols[0, m, e]
-                weights = weigh(q_expand[(col // 2) % 2, row], k_early[col // CHUNK, col % 2])
-            else:
-                weights = weigh(q_expand[upper, row], kx[m, i])
-            pair = vx[m, i]
+            upper, pair = e % 2, vx[m, e // 2]
+            weights = weigh(q_expand[upper, exp_rows[0, m, e]], kx[m, e // 2])
             if upper:
                 part = jnp.dot(weights, jnp.where(low, jnp.ones_like(pair), pair), preferred_element_type=F32)
             else:
                 part = half_turn(jnp.dot(weights, jnp.where(low, pair, jnp.ones_like(pair)), preferred_element_type=F32))
-            seg[m, e] = part + seg[m, prev[m * ET + e]]
-
-    for copy in forwards:
-        copy.wait()
-    order = tuple(reversed(SENDING))
-    for m in order:
-        if m == order[-1]:
-            def gather_totals(t, carry):
-                total = acc[t]
-                for m in order[:-1]:
-                    total += seg[m, last[m * RT + t]]
-                acc[t] = total
-                return carry
-
-            lax.fori_loop(0, RT, gather_totals, 0)
-        if m != EARLY:
-            kx_copies[m].wait()
-        vx_copies[m].wait()
-        expander(m)
+            parts.append(part)
+        for e in range(ET):
+            seg[m, e] = parts[e] + seg[m, prev[m * ET + e]]
+        return carry
+
+    def gather_totals(t, carry):
+        total = acc[t]
+        for m in range(MATCH):
+            if m != final:
+                total += seg[m, last[m * RT + t]]
+        acc[t] = total
+        return carry
+
+    final = TAKING * (MATCH - 1) % MATCH
+    lax.fori_loop(0, MATCH, expander, 0)
 
     def finish(z):
         tiles = []
         for i in range(CHUNK):
             t = CHUNK * z + i
-            total = acc[t] + seg[order[-1], last[order[-1] * RT + t]]
+            total = acc[t] + seg[final, last[final * RT + t]]
             tiles.append(total / half_turn(total))
         top = half_turn(jnp.concatenate(tiles[:2], axis=0))
         bottom = jnp.concatenate(tiles[2:], axis=0)
         send_o[z] = jnp.where(low_half, top, bottom).astype(BF16).reshape(2, TILE, TILE)
 
-    o_copies = z_copies(send_o, o_in.at[me], o_ss, o_rs)
-    for i in reversed(range(len(DISTANCES))):
-        finish(around(DISTANCES[i]))
-        o_copies[i].start()
-    finish(me)
+    def send_result(k, carry):
+        i = jnp.maximum(STEPS - 1 - k, 0)
+        z = jnp.where(k < STEPS, around(distance(i)), me)
+        finish(z)
+
+        @pl.when(k < STEPS)
+        def _():
+            z_copy(i, send_o, o_in, o_sems).start()
+
+        return carry
+
+    lax.fori_loop(0, HEADS, send_result, 0)
     o_in[me] = send_o[me]
-    for copy in o_copies:
-        copy.wait()
-    for copy in k_copies + v_copies + q_copies:
-        copy.wait_send()
+
+    def close(i, source):
+        z_copy(i, send_o, o_in, o_sems).wait()
+        z_copy(i, send_k, k_in, k_sems).wait_send()
+        z_copy(i, send_v, v_in, v_sems).wait_send()
+        z_copy(i, send_q, q_in, q_sems).wait_send()
+
+    steps(close)
     for pair in range(HEADS // 2):
         a, b = (o_in[2 * pair + i].reshape(half, TILE).astype(F32) for i in range(2))
         out[:half, pair * TILE : (pair + 1) * TILE] = jnp.where(low_half, a, half_turn(b)).astype(BF16)
@@ -331,7 +388,7 @@
     smem = pl.BlockSpec(memory_space=pltpu.SMEM)
     vmem = pl.BlockSpec(memory_space=pltpu.VMEM)
     hbm = pl.BlockSpec(memory_space=pltpu.HBM)
-    n = len(DISTANCES)
+    n = STEPS
     dma = pltpu.SemaphoreType.DMA
     packed = pltpu.VMEM((HEADS, 2, TILE, TILE), BF16)
     block = pltpu.VMEM((RT + 2 * HT, TILE, TILE), BF16)
@@ -355,6 +412,7 @@
             pltpu.VMEM((2, RT, TILE, TILE), BF16),
             pltpu.VMEM((MATCH, MATCH, ET), jnp.int32),
             pltpu.SMEM((MATCH, MATCH, ET), jnp.int32),
+            pltpu.VMEM((RT, TILE, TILE), BF16),
             pairs, pairs, pairs, pairs,
             pltpu.VMEM((RT, TILE, TILE), F32),
             pltpu.VMEM((MATCH, ET + 1, TILE, TILE), F32),

time: 85.6 us -> 80.9 us (0.945)
  Pallas kernels: 83.5 us -> 78.8 us
    pallas_call x1, Pallas kernels: 83.5 us -> 78.8 us  [local(): pl.pallas_call(kernel, name='exphormer', out_shape=jax.ShapeDtypeStruct((...]
where the time goes in v5:
time: 80.9 us; the launch traced here: 80.7 us
  Pallas kernels  78.8 us (97%)
  local copies, waits for them, and re-layouts  1.87 us (2%)
    pallas_call x1, Pallas kernels, local(): pl.pallas_call(kernel, name='exphormer', out_shape=jax.ShapeDtypeStruct((...  78.8 us
    unnamed x1, local copies, waits for them, and re-layouts  1.87 us

profile of v5, /device:TPU:1, one launch (start us, length us, event | category | flops | bytes accessed | tf_op | source)
XLA Modules:
  0.0 80.7 jit_solution(13788862679717323605)
XLA Ops:
  0.0 78.8 %exphormer.1 = bf16[512,512]{1,0:T(8,128)(2,1)} custom-call(s32[8,32]{1,0:T(8,128)} %bitcast.5, s32[1,4,16]{2,1,0:T(4,128)} %exp_rows.1, s32[1,4,16]{2,1,0:T(4,128)} %exp_cols.1, bf16[512,512]{1,0:T(8,128)(2,1)} %feat_hbm.1, bf16[512,512]{1,0:T(8,128)(2,1)} %w_q_hbm.1, bf16[512,2,512]{2,1,0:T(2,128)(2,1)} %w_kv_hbm.1, f32[1,64]{1,0:T(1,128)} %bitcast.6, ...), custom_call_target="tpu_custom_call" | custom-call | tf_op jit(solution)/shard_map/exphormer/pallas_call | solution.py:397
  78.8 1.9 %copy.10 = bf16[512,512]{1,0:T(8,128)(2,1)} copy(bf16[512,512]{1,0:T(8,128)(2,1)} %exphormer.1) | data formatting | bytes 1048576

commit v6 on v5

--- a/solution.py
+++ b/solution.py
@@ -30,6 +30,7 @@
 
 
 STEPS = HEADS - 1
+AHEAD = 4
 
 
 def distance(i):
@@ -46,6 +47,10 @@
 
 def contract_last(a, b):
     return lax.dot_general(a, b, (((1,), (1,)), ((), ())), preferred_element_type=F32)
+
+
+def with_ones(kv):
+    return jnp.where(low_lanes(kv.shape[0]), jnp.ones_like(kv), kv)
 
 
 def weigh(q, keys):
@@ -56,7 +61,7 @@
     local_cols, exp_rows, exp_cols, feat_hbm, w_q_hbm, w_kv_hbm, e_local, e_expand, cols_out, out,
     feat, w_q, w_kv, send_k, send_v, send_q, send_o, k_in, v_in, q_in, o_in, k_early,
     keys, values, turned_values, halo_out, halo_in, q_local, q_expand, cols_in, cols_smem, keys_early,
-    send_kx, send_vx, kx, vx, acc, seg, edges, last, prev,
+    send_kx, send_vx, kx, vx, acc, seg, edges, last, prev, listed,
     in_sem, k_ss, k_rs, v_ss, v_rs, q_ss, q_rs, o_ss, o_rs,
     c_ss, c_rs, c_local, h_ss, h_rs, kx_ss, kx_rs, vx_ss, vx_rs, y_ss, y_rs,
 ):
@@ -154,19 +159,25 @@
 
     take_keys(me)
 
+    def take_cols():
+        local = [pltpu.make_async_copy(cols_in.at[m], cols_smem.at[m], c_local.at[m]) for m in SENDING]
+        for m, copy in zip(SENDING, local):
+            col_copies[m].wait()
+            copy.start()
+        for copy in local:
+            copy.wait()
+
     def on_keys(i, source):
         z_copy(i, send_k, k_in, k_sems).wait_recv()
         z_copy(i, send_v, v_in, v_sems).start()
         forward(i, k_in, source).start()
         take_keys(source)
 
+        @pl.when(i == STEPS // 2)
+        def _():
+            take_cols()
+
     steps(on_keys)
-
-    for m in SENDING:
-        col_copies[m].wait()
-        local = pltpu.make_async_copy(cols_in.at[m], cols_smem.at[m], c_local.at[m])
-        local.start()
-        local.wait()
 
     def kx_copy(m):
         return remote(send_kx.at[m], kx.at[m], kx_ss.at[m], kx_rs.at[m], matched(m))
@@ -187,6 +198,7 @@
         copy.wait()
     project(lambda at: w_q[:, at], send_q)
     q_in[me] = send_q[me]
+    steps(lambda i, source: z_copy(i, send_q, q_in, q_sems).start())
 
     for row, source in ((0, e_local), (1, e_expand)):
         scaled = source[...] * (1.0 / math.sqrt(HDIM))
@@ -194,6 +206,9 @@
         edges[row : row + 1, HDIM:] = scaled
     for m in range(MATCH):
         seg[m, NONE] = jnp.zeros((TILE, TILE), F32)
+    for at in (0, HT + RT):
+        keys[pl.ds(at, HT)] = jnp.zeros((HT, TILE, TILE), BF16)
+        values[pl.ds(at, HT)] = jnp.zeros((HT, TILE, TILE), BF16)
 
     def link(m, carry):
         rows = [exp_rows[0, m, e] for e in range(ET)]
@@ -212,6 +227,12 @@
             for e in range(ET):
                 found = jnp.where(exp_rows[0, m, e] == t, e, found)
             last[m * RT + t] = found
+        for h in range(2 * HT):
+            inside = node > 0 if h < HT else node < NODES - 1
+            times = jnp.int32(0)
+            for slot in range(LPR):
+                times += jnp.where(local_cols[slot, t] == (h if h < HT else RT + h), 1, 0)
+            listed[h * RT + t] = jnp.where(inside, times, 0)
         return carry
 
     lax.fori_loop(0, RT, find, 0)
@@ -244,7 +265,6 @@
 
     def on_values(i, source):
         z_copy(i, send_v, v_in, v_sems).wait_recv()
-        z_copy(i, send_q, q_in, q_sems).start()
         take_values(source)
 
     steps(on_values)
@@ -252,18 +272,6 @@
     for m in SENDING:
         pick(m, turned_values, send_vx)
         vx_copy(m).start()
-
-    forward(STEPS, send_k, me).wait()
-    spread(k_early[me], keys_early, CHUNK * me)
-
-    def on_forwarded(i, source):
-        forward(i, k_in, source).wait()
-        spread(k_early[source], keys_early, CHUNK * source)
-
-    steps(on_forwarded)
-    for i in range(ET // 2):
-        one, other = exp_cols[0, EARLY, 2 * i], exp_cols[0, EARLY, 2 * i + 1]
-        kx[EARLY, i] = jnp.where(low, keys_early[one], keys_early[other ^ 2])
 
     def unpack(z):
         packed = q_in[z].reshape(half, TILE).astype(F32)
@@ -282,41 +290,48 @@
                     q_expand[1, pl.ds(CHUNK * z + 2 * (1 - part), 2)] = upper
 
     def local_tiles(z):
+        totals = []
         for i in range(CHUNK):
             t = CHUNK * z + i
             slots = [local_cols[s, t] for s in range(LPR)]
             some_keys = jnp.concatenate([keys[c] for c in slots], axis=0)
             some_values = jnp.concatenate([values[c] for c in slots], axis=0)
-            acc[t] = jnp.dot(weigh(q_local[t], some_keys), some_values, preferred_element_type=F32)
-
-    for copy in halo_copies:
-        copy.wait()
-    inside = (jnp.where(node > 0, 1.0, 0.0).astype(F32), jnp.where(node < NODES - 1, 1.0, 0.0).astype(F32))
-    for which, at in ((0, 0), (1, HT + RT)):
-        for i in range(HT):
-            keys[at + i] = halo_in[which, i]
-            values[at + i] = (jnp.where(low, 1.0, halo_in[which, i].astype(F32)) * inside[which]).astype(BF16)
+            totals.append(jnp.dot(weigh(q_local[t], some_keys), some_values, preferred_element_type=F32))
+        for i in range(CHUNK):
+            acc[CHUNK * z + i] = totals[i]
+
+    def chunk_of(k):
+        return jnp.where(k > 0, around(HEADS - distance(jnp.maximum(k - 1, 0))), me)
 
     def on_queries(k, carry):
-        i = jnp.maximum(k - 1, 0)
-
         @pl.when(k > 0)
         def _():
-            z_copy(i, send_q, q_in, q_sems).wait_recv()
-
-        z = jnp.where(k > 0, around(HEADS - distance(i)), me)
-        unpack(z)
-        local_tiles(z)
+            z_copy(jnp.maximum(k - 1, 0), send_q, q_in, q_sems).wait_recv()
+
+        unpack(chunk_of(k))
+
+        @pl.when(k < AHEAD)
+        def _():
+            local_tiles(chunk_of(k))
+
         return carry
 
     lax.fori_loop(0, HEADS, on_queries, 0)
+
+    forward(STEPS, send_k, me).wait()
+    spread(k_early[me], keys_early, CHUNK * me)
+
+    def on_forwarded(i, source):
+        forward(i, k_in, source).wait()
+        spread(k_early[source], keys_early, CHUNK * source)
+
+    steps(on_forwarded)
+    for i in range(ET // 2):
+        one, other = exp_cols[0, EARLY, 2 * i], exp_cols[0, EARLY, 2 * i + 1]
+        kx[EARLY, i] = jnp.where(low, keys_early[one], keys_early[other ^ 2])
 
     def expander(k, carry):
         m = TAKING * k % MATCH
-
-        @pl.when(k == MATCH - 1)
-        def _():
-            lax.fori_loop(0, RT, gather_totals, 0)
 
         @pl.when(m != EARLY)
         def _():
@@ -336,22 +351,50 @@
             seg[m, e] = parts[e] + seg[m, prev[m * ET + e]]
         return carry
 
-    def gather_totals(t, carry):
-        total = acc[t]
-        for m in range(MATCH):
-            if m != final:
-                total += seg[m, last[m * RT + t]]
-        acc[t] = total
-        return carry
-
-    final = TAKING * (MATCH - 1) % MATCH
-    lax.fori_loop(0, MATCH, expander, 0)
+    lax.fori_loop(0, MATCH - 2, expander, 0)
+
+    for copy in halo_copies:
+        copy.wait()
+    outer = halo_in[...].reshape(2 * HT * TILE, TILE)
+    outer_values = with_ones(outer)
+
+    def halo_tiles(k, carry):
+        z = chunk_of(k)
+        weights = weigh(q_local[pl.ds(CHUNK * z, CHUNK)].reshape(CHUNK * TILE, TILE), outer)
+        parts = [
+            jnp.dot(weights[:, h * TILE : (h + 1) * TILE], outer_values[h * TILE : (h + 1) * TILE], preferred_element_type=F32)
+            for h in range(2 * HT)
+        ]
+        for i in range(CHUNK):
+            t = CHUNK * z + i
+            total = acc[t]
+            for h in range(2 * HT):
+                total += parts[h][i * TILE : (i + 1) * TILE] * listed[h * RT + t].astype(F32)
+            acc[t] = total
+        return carry
+
+    lax.fori_loop(0, AHEAD, halo_tiles, 0)
+    inside = (jnp.where(node > 0, 1.0, 0.0).astype(F32), jnp.where(node < NODES - 1, 1.0, 0.0).astype(F32))
+    for which, at in ((0, 0), (1, HT + RT)):
+        for i in range(HT):
+            keys[at + i] = halo_in[which, i]
+            values[at + i] = (with_ones(halo_in[which, i]).astype(F32) * inside[which]).astype(BF16)
+
+    def local_rest(k, carry):
+        local_tiles(chunk_of(k))
+        return carry
+
+    lax.fori_loop(AHEAD, HEADS, local_rest, 0)
+
+    lax.fori_loop(MATCH - 2, MATCH, expander, 0)
 
     def finish(z):
         tiles = []
         for i in range(CHUNK):
             t = CHUNK * z + i
-            total = acc[t] + seg[final, last[final * RT + t]]
+            total = acc[t]
+            for m in range(MATCH):
+                total += seg[m, last[m * RT + t]]
             tiles.append(total / half_turn(total))
         top = half_turn(jnp.concatenate(tiles[:2], axis=0))
         bottom = jnp.concatenate(tiles[2:], axis=0)
@@ -419,6 +462,7 @@
             pltpu.VMEM((2, TILE), F32),
             pltpu.SMEM((MATCH * RT,), jnp.int32),
             pltpu.SMEM((MATCH * ET,), jnp.int32),
+            pltpu.SMEM((2 * HT * RT,), jnp.int32),
             dma((3, PIECES)),
             dma((n,)), dma((n,)), dma((n,)), dma((n,)), dma((n,)), dma((n,)), dma((n,)), dma((n,)),
             dma((MATCH,)), dma((MATCH,)), dma((MATCH,)), dma((2,)), dma((2,)),

time: 80.9 us -> 79.3 us (0.980)
  the two profiles are of different devices: /device:TPU:1 before, /device:TPU:6 now
where the time goes in v6:
time: 79.3 us; the launch traced here: 79 us
  Pallas kernels  77.1 us (97%)
  local copies, waits for them, and re-layouts  1.87 us (2%)
    pallas_call x1, Pallas kernels, local(): pl.pallas_call(kernel, name='exphormer', out_shape=jax.ShapeDtypeStruct((...  77.1 us
    unnamed x1, local copies, waits for them, and re-layouts  1.87 us

profile of v6, /device:TPU:6, one launch (start us, length us, event | category | flops | bytes accessed | tf_op | source)
XLA Modules:
  0.0 79.0 jit_solution(8415510022670922200)
XLA Ops:
  0.0 77.1 %exphormer.1 = bf16[512,512]{1,0:T(8,128)(2,1)} custom-call(s32[8,32]{1,0:T(8,128)} %bitcast.5, s32[1,4,16]{2,1,0:T(4,128)} %exp_rows.1, s32[1,4,16]{2,1,0:T(4,128)} %exp_cols.1, bf16[512,512]{1,0:T(8,128)(2,1)} %feat_hbm.1, bf16[512,512]{1,0:T(8,128)(2,1)} %w_q_hbm.1, bf16[512,2,512]{2,1,0:T(2,128)(2,1)} %w_kv_hbm.1, f32[1,64]{1,0:T(1,128)} %bitcast.6, ...), custom_call_target="tpu_custom_call" | custom-call | tf_op jit(solution)/shard_map/exphormer/pallas_call | solution.py:440
  77.1 1.9 %copy.10 = bf16[512,512]{1,0:T(8,128)(2,1)} copy(bf16[512,512]{1,0:T(8,128)(2,1)} %exphormer.1) | data formatting | bytes 1048576

commit v7 on v6

--- a/solution.py
+++ b/solution.py
@@ -159,6 +159,8 @@
 
     take_keys(me)
 
+    steps(lambda i, source: z_copy(i, send_v, v_in, v_sems).start())
+
     def take_cols():
         local = [pltpu.make_async_copy(cols_in.at[m], cols_smem.at[m], c_local.at[m]) for m in SENDING]
         for m, copy in zip(SENDING, local):
@@ -169,7 +171,6 @@
 
     def on_keys(i, source):
         z_copy(i, send_k, k_in, k_sems).wait_recv()
-        z_copy(i, send_v, v_in, v_sems).start()
         forward(i, k_in, source).start()
         take_keys(source)
 

time: 79.3 us -> 79.6 us (level)
  the two profiles are of different devices: /device:TPU:6 before, /device:TPU:1 now
where the time goes in v7:
time: 79.6 us; the launch traced here: 78.7 us
  Pallas kernels  76.8 us (96%)
  local copies, waits for them, and re-layouts  1.87 us (2%)
    pallas_call x1, Pallas kernels, local(): pl.pallas_call(kernel, name='exphormer', out_shape=jax.ShapeDtypeStruct((...  76.8 us
    unnamed x1, local copies, waits for them, and re-layouts  1.87 us

profile of v7, /device:TPU:1, one launch (start us, length us, event | category | flops | bytes accessed | tf_op | source)
XLA Modules:
  0.0 78.7 jit_solution(13917482651259165562)
XLA Ops:
  0.0 76.8 %exphormer.1 = bf16[512,512]{1,0:T(8,128)(2,1)} custom-call(s32[8,32]{1,0:T(8,128)} %bitcast.5, s32[1,4,16]{2,1,0:T(4,128)} %exp_rows.1, s32[1,4,16]{2,1,0:T(4,128)} %exp_cols.1, bf16[512,512]{1,0:T(8,128)(2,1)} %feat_hbm.1, bf16[512,512]{1,0:T(8,128)(2,1)} %w_q_hbm.1, bf16[512,2,512]{2,1,0:T(2,128)(2,1)} %w_kv_hbm.1, f32[1,64]{1,0:T(1,128)} %bitcast.6, ...), custom_call_target="tpu_custom_call" | custom-call | tf_op jit(solution)/shard_map/exphormer/pallas_call | solution.py:441
  76.8 1.9 %copy.10 = bf16[512,512]{1,0:T(8,128)(2,1)} copy(bf16[512,512]{1,0:T(8,128)(2,1)} %exphormer.1) | data formatting | bytes 1048576
